TPU v7x, 512 devices: a whole 4x4x16 slice. The times are simulated.
512 devices in a mesh: prefix: 32 (over x, y, core), sample: 16 (over z).
Axes of the slice: x: 4, y: 4, z: 16, core: 2. Of those that a mesh axis runs over, the one named last changes fastest.
Arguments:
- queries: bfloat16 [64, 8192], P('sample'), may hold values from -100 to 100
- pool_keys: bfloat16 [2048, 128, 1024], P(('prefix', 'sample')), may hold values from -6 to 6
- pool_values: bfloat16 [2048, 128, 1024], P(('prefix', 'sample')), may hold values from -6 to 6
- page_prompt: int32 [2048], P(('prefix', 'sample')), may hold values from -1 to 3, as said below
- suffix_keys: bfloat16 [64, 1024, 1024], P('sample', 'prefix'), may hold values from -6 to 6
- suffix_values: bfloat16 [64, 1024, 1024], P('sample', 'prefix'), may hold values from -6 to 6
- suffix_len: int32 [64], P('sample'), may hold values from 1 to 1024, as said below
Outputs:
- attention_out: bfloat16 [64, 8192], P('sample', 'prefix')
Inputs may be any that keep to these rules, and one draw needn't show every extreme that they name: `page_prompt`: each of the 4 prompts is held by exactly 256 slots; every other slot holds -1. `suffix_len`: the longest suffix is exactly 1024.
All inputs are finite; a program needn't handle non-finite values.
Results may differ from a plain program's by a relative error of at most 0.0065.
Values may be sent and summed in bfloat16 or wider, within the bound.
No kernel may reach another device: no remote copies, remote signals or barrier semaphores. Data moves between devices by JAX's collectives and lax.ppermute only.
A program may use at most 64 MiB of HBM per device.

v0:
```python
import math

import jax
import jax.numpy as jnp
from jax import lax
from jax.sharding import PartitionSpec as P

H = 64
KVH = 8
HD = 128
SPP = 16


NEG_FILL = -1e30


def body(queries, pool_keys, pool_values, page_prompt, suffix_keys, suffix_values, suffix_len):
    group_size = H // KVH
    score_scale = 1.0 / math.sqrt(HD)
    local_rows = queries.shape[0]
    slot_count = pool_keys.shape[0]
    suffix_span = suffix_keys.shape[1]
    highest = lax.Precision.HIGHEST
    every_query = lax.all_gather(queries, "sample", axis=0, tiled=True)
    rows_all = every_query.shape[0]
    prompts = rows_all // SPP
    query_grid = every_query.reshape(prompts, SPP, KVH, group_size, HD)
    safe_prompt = jnp.maximum(page_prompt, 0)
    onehot = page_prompt[:, None] == jnp.arange(prompts, dtype=jnp.int32)[None, :]
    live_slot = page_prompt >= 0
    slot_queries = jnp.take(query_grid, safe_prompt, axis=0)
    page_keys = pool_keys.reshape(slot_count, pool_keys.shape[1], KVH, HD)
    page_values = pool_values.reshape(slot_count, pool_values.shape[1], KVH, HD)
    prefix_scores = (
        jnp.einsum("jsagd,jtad->jsagt", slot_queries, page_keys, preferred_element_type=jnp.float32)
        * score_scale
    )
    slot_peak = prefix_scores.max(-1)
    prompt_peak = jnp.max(
        jnp.where(onehot[:, :, None, None, None], slot_peak[:, None], NEG_FILL), axis=0
    )
    row_peak = prompt_peak.reshape(rows_all, KVH, group_size)
    own_queries = queries.reshape(local_rows, KVH, group_size, HD)
    suffix_key_rows = suffix_keys.reshape(local_rows, suffix_span, KVH, HD)
    suffix_value_rows = suffix_values.reshape(local_rows, suffix_span, KVH, HD)
    positions = lax.axis_index("prefix") * suffix_span + jnp.arange(suffix_span, dtype=jnp.int32)
    live_mask = (positions[None, :] < suffix_len[:, None])[:, None, None, :]
    suffix_scores = (
        jnp.einsum(
            "bagd,btad->bagt", own_queries, suffix_key_rows, preferred_element_type=jnp.float32
        )
        * score_scale
    )
    suffix_scores = jnp.where(live_mask, suffix_scores, NEG_FILL)
    row_start = lax.axis_index("sample") * local_rows
    own_peak = lax.dynamic_slice_in_dim(row_peak, row_start, local_rows, 0)
    row_peak = lax.dynamic_update_slice_in_dim(
        row_peak, jnp.maximum(own_peak, suffix_scores.max(-1)), row_start, 0
    )
    peak = lax.pmax(row_peak, ("prefix", "sample"))
    peak_grid = peak.reshape(prompts, SPP, KVH, group_size)
    slot_peaks = jnp.take(peak_grid, safe_prompt, axis=0)
    prefix_weights = jnp.exp(prefix_scores - slot_peaks[..., None])
    prefix_weights = jnp.where(live_slot[:, None, None, None, None], prefix_weights, 0.0)
    slot_denominator = prefix_weights.sum(-1)
    slot_numerator = jnp.einsum(
        "jsagt,jtad->jsagd",
        prefix_weights.astype(jnp.bfloat16),
        page_values,
        preferred_element_type=jnp.float32,
    )
    onehot_float = onehot.astype(jnp.float32)
    numerator = jnp.einsum(
        "jp,jsagd->psagd", onehot_float, slot_numerator, precision=highest
    ).reshape(rows_all, H, HD)
    denominator = jnp.einsum(
        "jp,jsag->psag", onehot_float, slot_denominator, precision=highest
    ).reshape(rows_all, H)
    suffix_peak = lax.dynamic_slice_in_dim(peak, row_start, local_rows, 0)
    suffix_weights = jnp.where(live_mask, jnp.exp(suffix_scores - suffix_peak[..., None]), 0.0)
    suffix_numerator = jnp.einsum(
        "bagt,btad->bagd",
        suffix_weights.astype(jnp.bfloat16),
        suffix_value_rows,
        preferred_element_type=jnp.float32,
    )
    own_numerator = lax.dynamic_slice_in_dim(
        numerator, row_start, local_rows, 0
    ) + suffix_numerator.reshape(local_rows, H, HD)
    own_denominator = lax.dynamic_slice_in_dim(
        denominator, row_start, local_rows, 0
    ) + suffix_weights.sum(-1).reshape(local_rows, H)
    numerator = lax.dynamic_update_slice_in_dim(numerator, own_numerator, row_start, 0)
    denominator = lax.dynamic_update_slice_in_dim(denominator, own_denominator, row_start, 0)
    numerator, denominator = (
        lax.psum_scatter(numerator, "sample", scatter_dimension=0, tiled=True),
        lax.psum_scatter(denominator, "sample", scatter_dimension=0, tiled=True),
    )
    numerator, denominator = (
        lax.psum_scatter(numerator, "prefix", scatter_dimension=1, tiled=True),
        lax.psum_scatter(denominator, "prefix", scatter_dimension=1, tiled=True),
    )
    mixed = numerator / denominator[..., None]
    return mixed.astype(jnp.bfloat16).reshape(local_rows, -1)


def solution(mesh):
    placed = (
        P("sample", None),
        P(("prefix", "sample"), None, None),
        P(("prefix", "sample"), None, None),
        P(("prefix", "sample")),
        P("sample", "prefix", None),
        P("sample", "prefix", None),
        P("sample"),
    )
    return jax.shard_map(
        body, mesh=mesh, in_specs=placed, out_specs=P("sample", "prefix"), check_vma=False
    )
```

profile of v0, /device:TPU:1, one launch (start us, length us, event | category | flops | bytes accessed | tf_op | source)
XLA Modules:
  0.0 542.7 jit_solution(9295658461145735650)
XLA Ops:
  8.6 1.5 copy.95
  11.7 1.3 fusion.38
  13.0 1.1 bitcast_bitcast_fusion.1
  15.2 61.2 %all-gather.3.cloned.1.call-done = bf16[16,4,8192]{2,1,0:T(4,128)(2,1)} async-done(((bf16[1,4,8192]{2,1,0:T(4,128)(2,1)}), bf16[16,4,8192]{2,1,0:T(4,128)(2,1)}) %all-gather.3.cloned.1.call-update) | async-done | bytes 1048592 | tf_op jit(solution)/shard_map/all_gather | solution.py:24
  76.4 2.1 reshape.98
  79.4 3.0 bitcast_reduce_fusion
  82.4 1.8 copy.66
  85.9 1.6 reshape.100
  87.6 1.4 constant_dynamic-slice_fusion.1
  89.0 1.5 copy.92
  90.5 1.3 max.9
  91.8 1.4 copy.70
  93.2 1.4 dynamic_update_slice.9
  94.6 111.5 %pmax.7 = f32[64,8,8]{0,2,1:T(8,128)} all-reduce(f32[64,8,8]{0,2,1:T(8,128)} %dynamic_update_slice.9), channel_id=1, replica_groups=mesh['prefix'=32,'sample'=16] {'prefix','sample'}, use_global_device_ids=true, to_apply=%region_3.4 | all-reduce | flops 4096 | bytes 32768 | tf_op jit(solution)/shard_map/pmax | solution.py:60
  206.1 1.4 constant_dynamic-slice_fusion
  207.5 1.5 reshape.103
  209.9 1.6 copy.71
  211.5 2.2 gather_fusion.1
  213.7 1.6 broadcast_select_fusion.1
  215.4 1.8 copy.72
  217.1 2.8 convolution_bitcast_fusion
  219.9 3.2 fusion.2
  223.2 1.6 copy.75
  224.8 1.8 fusion.7
  226.7 1.3 dynamic-slice.2
  228.1 1.3 dynamic-slice
  231.1 1.4 fusion.4
  233.3 41.7 %all-reduce.1 = f32[64,64]{0,1:T(8,128)S(1)} all-reduce(f32[64,64]{0,1:T(8,128)S(1)} %dynamic_update_slice.11), channel_id=4, replica_groups=mesh['prefix'=32,'sample'=16] {'sample'}, use_global_device_ids=true, to_apply=%region_8.9.clone | all-reduce | flops 4096 | bytes 32768
  275.0 130.1 %all-reduce.2 = f32[4,64]{0,1:T(8,128)S(1)} all-reduce(f32[4,64]{0,1:T(8,128)S(1)} %constant_dynamic-slice_fusion.3), channel_id=5, replica_groups=mesh['prefix'=32,'sample'=16] {'prefix'}, use_global_device_ids=true, to_apply=%region_9.10.clone | all-reduce | flops 256 | bytes 2048
  405.1 1.6 copy.78
  406.8 128.1 %all-reduce.5.cloned.1.call-done = f32[4,64,128]{2,0,1:T(4,128)} async-done(((f32[4,64,128]{2,0,1:T(4,128)}), f32[4,64,128]{2,0,1:T(4,128)}) %all-reduce.5.cloned.1.call-update) | async-done | bytes 131088
  534.9 1.3 fusion.34
  (51 shorter events, 9.5 us)
Async XLA Ops:
  6.5 218.3 %copy-start = (bf16[4,32,1024]{2,1,0:T(8,128)(2,1)S(1)}, bf16[4,32,1024]{2,1,0:T(8,128)(2,1)}, u32[]{:S(2)}) copy-start(bf16[4,32,1024]{2,1,0:T(8,128)(2,1)} %param.12) | copy-start | bytes 786436
  6.5 3.6 copy-start.3
  6.5 69.8 %all-gather.3.cloned.1.call-start = ((), (), s32[]{:S(2)}) async-start(), calls=%async_computation.2 | async-start | bytes 1114112 | tf_op jit(solution)/shard_map/all_gather | solution.py:24
  7.3 397.8 %reduce-scatter.3.cloned.1.call-start = ((), (), s32[]{:S(2)}) async-start(), calls=%async_computation.1 | async-start | bytes 2228224 | tf_op jit(solution)/shard_map/reduce_scatter | solution.py:96
  8.6 1.8 copy-start.6
  8.6 3.0 copy-start.10
  11.7 3.4 copy-start.4
  82.3 134.8 %copy-start.1 = (bf16[4,128,8,128,1]{3,2,1,0,4:T(8,128)(2,1)S(1)}, bf16[4,128,8,128,1]{3,2,1,0,4:T(8,128)(2,1)}, u32[]{:S(2)}) copy-start(bf16[4,128,8,128,1]{3,2,1,0,4:T(8,128)(2,1)} %bitcast_bitcast_fusion) | copy-start | bytes 3145732
  217.1 2.8 copy-start.7
  223.2 1.7 copy-start.5
  224.8 6.3 %copy-start.2 = (f32[4,16,8,8]{3,1,2,0:T(8,128)S(1)}, f32[4,16,8,8]{3,1,2,0:T(8,128)}, u32[]{:S(2)}) copy-start(f32[4,16,8,8]{3,1,2,0:T(8,128)} %copy.72) | copy-start | bytes 49156
  224.8 6.3 %copy-start.9 = (pred[4]{0:T(512)(128)(4,1)S(1)}, pred[4]{0:T(512)(128)(4,1)}, u32[]{:S(2)}) copy-start(pred[4]{0:T(512)(128)(4,1)} %get-tuple-element.5) | copy-start | bytes 16
  226.7 5.9 %copy-start.8 = (s32[4]{0:T(128)S(1)}, s32[4]{0:T(128)}, u32[]{:S(2)}) copy-start(s32[4]{0:T(128)} %param.10) | copy-start | bytes 52
  226.7 308.2 %all-reduce.5.cloned.1.call-start = ((), (), s32[]{:S(2)}) async-start(), calls=%async_computation.3 | async-start | bytes 262144
Sparse Core Ops, SparseCore 0:
  9.4 66.8 all-gather.2
  226.8 57.0 reduce-scatter.2
  406.9 127.9 all-reduce.4
where the time goes:
time: 544 us; the launch traced here: 543 us
  blocking collectives  283 us (52%)
  waiting for transfers between devices  190 us (35%)
  local copies, waits for them, and re-layouts  33.5 us (6%)
  between operations  14.6 us (3%)
  matrix products  12.4 us (2%)
  other arithmetic  8.9 us (2%)
    unnamed x2, blocking collectives  172 us
    unnamed x4, waiting for transfers between devices  129 us
    pmax x1, blocking collectives, body(): peak = lax.pmax(row_peak, ('prefix', 'sample'))  111 us
    all_gather x1, waiting for transfers between devices, body(): every_query = lax.all_gather(queries, 'sample', axis=0, tiled=True)  61.2 us
  transfers between devices with their start and end apart: 3, of which 2 were waited for; matrix products, arithmetic and copies ran while one was open for 2% of the time, Pallas kernels for 0%

commit v1 on v0

v1 whole, which is shorter than its diff:
```python
import math

import jax
import jax.numpy as jnp
from jax import lax
from jax.experimental import pallas as pl
from jax.experimental.pallas import tpu as pltpu
from jax.sharding import PartitionSpec as P

H = 64
KVH = 8
HD = 128
PAGE = 128
SPP = 16
PROMPTS = 4
CORES = 2
OWN = 4
SPAN = 32
PLANE = 16
DEPTH = 16
ROWS = 128
HEAD_ROWS = 64
STAT_ROWS = 32
BLOCK_ROWS = ROWS + STAT_ROWS
SEND_ROWS = 2 * PAGE + 2 * SPAN + 16
NEG = -1e30
MIB = 1 << 20
SCALE = math.log2(math.e) / math.sqrt(HD)
F32 = jnp.float32
BF16 = jnp.bfloat16


def stage_kernel(page_prompt, queries, pool_keys, pool_values, suffix_keys, suffix_values,
                 query_out, send_out, sems):
    core = lax.rem(lax.axis_index("prefix"), CORES)
    pieces = ((pool_keys, 0, PAGE), (pool_values, PAGE, PAGE),
              (suffix_keys, 2 * PAGE, SPAN), (suffix_values, 2 * PAGE + SPAN, SPAN))
    copies = [
        pltpu.make_async_copy(src, send_out.at[:, pl.ds(start, rows), :], sems.at[i])
        for i, (src, start, rows) in enumerate(pieces)
    ]
    for copy in copies:
        copy.start()
    for slot in range(OWN):
        mark = jnp.full((16, KVH * HD), page_prompt[slot], jnp.int32)
        send_out[slot, pl.ds(2 * PAGE + 2 * SPAN, 16), :] = mark.astype(F32).astype(BF16)
    for a in range(KVH):
        parts = []
        for half in range(2):
            for mate in range(2):
                head = a * 8 + half * 4 + mate
                column = pl.multiple_of(head * HD + core * (2 * HD), HD)
                parts.append(queries[:, pl.ds(column, HD)].astype(F32))
        rows = jnp.concatenate(parts, axis=0).astype(BF16)
        for plane in range(DEPTH):
            query_out[plane, pl.ds(a * 16, 16), :] = rows
    for copy in copies:
        copy.wait()


def attend_kernel(page_prompt, suffix_len, queries_hbm, keys_hbm, values_hbm, suffix_keys_hbm,
                  suffix_values_hbm, got_hbm, out, queries, keys, values, suffix_keys,
                  suffix_values, marks, prompts, scores, top, peak, total, acc, sems):
    prefix = lax.axis_index("prefix")
    plane = lax.axis_index("sample")
    pairs = (
        (got_hbm.at[:, pl.ds(2 * PAGE + 2 * SPAN, 16), pl.ds(0, HD)], marks),
        (queries_hbm, queries),
        (keys_hbm, keys.at[pl.ds(0, OWN)]),
        (got_hbm.at[:, pl.ds(0, PAGE), :], keys.at[pl.ds(OWN, OWN)]),
        (suffix_keys_hbm, suffix_keys.at[0]),
        (got_hbm.at[:, pl.ds(2 * PAGE, SPAN), :], suffix_keys.at[1]),
        (values_hbm, values.at[pl.ds(0, OWN)]),
        (got_hbm.at[:, pl.ds(PAGE, PAGE), :], values.at[pl.ds(OWN, OWN)]),
        (suffix_values_hbm, suffix_values.at[0]),
        (got_hbm.at[:, pl.ds(2 * PAGE + SPAN, SPAN), :], suffix_values.at[1]),
    )
    copies = [pltpu.make_async_copy(src, dst, sems.at[i]) for i, (src, dst) in enumerate(pairs)]
    for copy in copies:
        copy.start()
    top[...] = jnp.full(top.shape, NEG, F32)
    total[...] = jnp.zeros(total.shape, F32)
    acc[...] = jnp.zeros(acc.shape, F32)

    copies[0].wait()
    for slot in range(OWN):
        prompts[slot] = page_prompt[slot]
        prompts[OWN + slot] = jnp.max(marks[slot].astype(F32)).astype(jnp.int32)

    own_prompt = lax.div(plane, 4)
    quarter = lax.rem(plane, 4)
    row = lax.broadcasted_iota(jnp.int32, (HEAD_ROWS, PAGE), 0)
    token = lax.broadcasted_iota(jnp.int32, (HEAD_ROWS, PAGE), 1)
    token_sample = token >> 5
    length = jnp.where(
        token_sample == 0, suffix_len[0],
        jnp.where(token_sample == 1, suffix_len[1],
                  jnp.where(token_sample == 2, suffix_len[2], suffix_len[3])))
    mine = ((row >> 4) == quarter) & ((row & 3) == token_sample)

    def live(part):
        owner = prefix if part == 0 else prefix + 1 - 2 * lax.rem(prefix, CORES)
        return mine & (owner * SPAN + (token & (SPAN - 1)) < length)

    def query_rows(prompt, a):
        rows = queries[pl.ds(prompt * 4, 4), pl.ds(a * 16, 16), :]
        return rows.reshape(HEAD_ROWS, HD)

    def dot_keys(prompt, a, key):
        return SCALE * lax.dot_general(
            query_rows(prompt, a), key, (((1,), (1,)), ((), ())), preferred_element_type=F32)

    for copy in copies[1:6]:
        copy.wait()

    @pl.loop(0, 2 * OWN)
    def _(slot):
        prompt = prompts[slot]

        @pl.when(prompt >= 0)
        def _():
            for a in range(KVH):
                s = dot_keys(prompt, a, keys[slot, :, pl.ds(a * HD, HD)])
                scores[slot, a] = s
                top[prompt, a] = jnp.maximum(top[prompt, a], s)

    for part in range(2):
        mask = live(part)
        for a in range(KVH):
            key = suffix_keys[part, :, :, pl.ds(a * HD, HD)].reshape(OWN * SPAN, HD)
            s = jnp.where(mask, dot_keys(own_prompt, a, key), NEG)
            scores[2 * OWN + part, a] = s
            top[own_prompt, a] = jnp.maximum(top[own_prompt, a], s)

    @pl.loop(0, PROMPTS)
    def _(prompt):
        for a in range(KVH):
            best = jnp.max(top[prompt, a], axis=1, keepdims=True)
            best = best.astype(BF16).astype(F32)
            peak[prompt, a] = jnp.broadcast_to(best, (HEAD_ROWS, HD))

    for copy in copies[6:]:
        copy.wait()

    @pl.loop(0, 2 * OWN)
    def _(slot):
        prompt = prompts[slot]

        @pl.when(prompt >= 0)
        def _():
            for a in range(KVH):
                w = jnp.exp2(scores[slot, a] - peak[prompt, a])
                total[prompt, a] += w
                acc[prompt, a] += jnp.dot(
                    w.astype(BF16), values[slot, :, pl.ds(a * HD, HD)],
                    preferred_element_type=F32)

    for part in range(2):
        mask = live(part)
        for a in range(KVH):
            value = suffix_values[part, :, :, pl.ds(a * HD, HD)].reshape(OWN * SPAN, HD)
            w = jnp.where(mask, jnp.exp2(scores[2 * OWN + part, a] - peak[own_prompt, a]), 0.0)
            total[own_prompt, a] += w
            acc[own_prompt, a] += jnp.dot(w.astype(BF16), value, preferred_element_type=F32)

    lane = lax.broadcasted_iota(jnp.int32, (HEAD_ROWS, HD), 1)

    @pl.loop(0, KVH)
    def _(a):
        stats = jnp.zeros((HEAD_ROWS, HD), F32)
        for prompt in range(PROMPTS):
            low = jnp.sum(total[prompt, a], axis=1, keepdims=True)
            high = low.astype(BF16).astype(F32)
            stats = jnp.where(lane == prompt, peak[prompt, a], stats)
            stats = jnp.where(lane == 4 + prompt, high, stats)
            stats = jnp.where(lane == 8 + prompt, low - high, stats)
        for half in range(2):
            def pick(tile):
                return jnp.concatenate(
                    [tile[q * 16 + half * 8:q * 16 + half * 8 + 8] for q in range(4)], axis=0)
            for prompt in range(PROMPTS):
                out[a * 2 + half, pl.ds(prompt * 32, 32), :] = pick(acc[prompt, a]).astype(BF16)
            out[a * 2 + half, pl.ds(ROWS, STAT_ROWS), :] = pick(stats).astype(BF16)


def plane_kernel(got, out):
    best = jnp.full((STAT_ROWS, HD), NEG, F32)
    for src in range(PLANE):
        best = jnp.maximum(best, got[src, pl.ds(ROWS, STAT_ROWS), :].astype(F32))
    denominator = jnp.zeros((STAT_ROWS, HD), F32)
    sums = [jnp.zeros((STAT_ROWS, HD), F32) for _ in range(PROMPTS)]
    for src in range(PLANE):
        stats = got[src, pl.ds(ROWS, STAT_ROWS), :].astype(F32)
        weight = jnp.exp2(jnp.minimum(stats - best, 0.0))
        part = pltpu.roll(stats, HD - 4, 1) + pltpu.roll(stats, HD - 8, 1)
        denominator = denominator + weight * part
        for prompt in range(PROMPTS):
            tile = got[src, pl.ds(prompt * 32, 32), :].astype(F32)
            sums[prompt] = sums[prompt] + tile * weight[:, prompt:prompt + 1]
    lane = lax.broadcasted_iota(jnp.int32, (8, HD), 1)
    for prompt in range(PROMPTS):
        for quarter in range(4):
            rows = slice(quarter * 8, quarter * 8 + 8)
            stat = jnp.where(lane == 0, best[rows, prompt:prompt + 1],
                             denominator[rows, prompt:prompt + 1])
            out[prompt * 4 + quarter, pl.ds(0, 8), :] = sums[prompt][rows]
            out[prompt * 4 + quarter, pl.ds(8, 8), :] = stat


def final_kernel(got, out):
    best = got[0, pl.ds(8, 8), :]
    for src in range(1, DEPTH):
        best = jnp.maximum(best, got[src, pl.ds(8, 8), :])
    best = best[:, 0:1]
    denominator = jnp.zeros((8, 1), F32)
    numerator = jnp.zeros((8, HD), F32)
    for src in range(DEPTH):
        stat = got[src, pl.ds(8, 8), :]
        weight = jnp.exp2(stat[:, 0:1] - best)
        denominator = denominator + weight * stat[:, 1:2]
        numerator = numerator + weight * got[src, pl.ds(0, 8), :]
    mixed = (numerator / denominator).astype(BF16)
    out[...] = jnp.concatenate([mixed[0:4], mixed[4:8]], axis=1)


SMEM = pl.BlockSpec(memory_space=pltpu.SMEM)
VMEM = pl.BlockSpec(memory_space=pltpu.VMEM)
ANY = pl.BlockSpec(memory_space=pl.ANY)


def body(queries, pool_keys, pool_values, page_prompt, suffix_keys, suffix_values, suffix_len):
    width = KVH * HD
    query_blocks, send = pl.pallas_call(
        stage_kernel,
        out_shape=(jax.ShapeDtypeStruct((DEPTH, ROWS, HD), BF16),
                   jax.ShapeDtypeStruct((OWN, SEND_ROWS, width), BF16)),
        in_specs=[SMEM, VMEM, ANY, ANY, ANY, ANY],
        out_specs=(VMEM, VMEM),
        scratch_shapes=[pltpu.SemaphoreType.DMA((4,))],
        compiler_params=pltpu.CompilerParams(vmem_limit_bytes=6 * MIB),
        name="stage",
    )(page_prompt, queries, pool_keys, pool_values, suffix_keys, suffix_values)
    got = lax.ppermute(send, "prefix", [(i, i ^ 1) for i in range(CORES * PLANE)])
    every_query = lax.all_to_all(query_blocks, "sample", 0, 0)
    partial = pl.pallas_call(
        attend_kernel,
        out_shape=jax.ShapeDtypeStruct((PLANE, BLOCK_ROWS, HD), BF16),
        in_specs=[SMEM, SMEM] + [ANY] * 6,
        out_specs=VMEM,
        scratch_shapes=[
            pltpu.VMEM((DEPTH, ROWS, HD), BF16),
            pltpu.VMEM((2 * OWN, PAGE, width), BF16),
            pltpu.VMEM((2 * OWN, PAGE, width), BF16),
            pltpu.VMEM((2, OWN, SPAN, width), BF16),
            pltpu.VMEM((2, OWN, SPAN, width), BF16),
            pltpu.VMEM((OWN, 16, HD), BF16),
            pltpu.SMEM((2 * OWN,), jnp.int32),
            pltpu.VMEM((2 * OWN + 2, KVH, HEAD_ROWS, PAGE), F32),
            pltpu.VMEM((PROMPTS, KVH, HEAD_ROWS, PAGE), F32),
            pltpu.VMEM((PROMPTS, KVH, HEAD_ROWS, HD), F32),
            pltpu.VMEM((PROMPTS, KVH, HEAD_ROWS, PAGE), F32),
            pltpu.VMEM((PROMPTS, KVH, HEAD_ROWS, HD), F32),
            pltpu.SemaphoreType.DMA((10,)),
        ],
        compiler_params=pltpu.CompilerParams(vmem_limit_bytes=16 * MIB),
        name="attend",
    )(page_prompt, suffix_len, every_query, pool_keys, pool_values, suffix_keys, suffix_values, got)
    same_core = [[chip * CORES + core for chip in range(PLANE)] for core in range(CORES)]
    partial = lax.all_to_all(partial, "prefix", 0, 0, axis_index_groups=same_core)
    summed = pl.pallas_call(
        plane_kernel,
        out_shape=jax.ShapeDtypeStruct((DEPTH, 16, HD), F32),
        in_specs=[VMEM],
        out_specs=VMEM,
        compiler_params=pltpu.CompilerParams(vmem_limit_bytes=4 * MIB),
        name="plane",
    )(partial)
    summed = lax.all_to_all(summed, "sample", 0, 0)
    return pl.pallas_call(
        final_kernel,
        out_shape=jax.ShapeDtypeStruct((OWN, 2 * HD), BF16),
        in_specs=[VMEM],
        out_specs=VMEM,
        compiler_params=pltpu.CompilerParams(vmem_limit_bytes=2 * MIB),
        name="final",
    )(summed)


def solution(mesh):
    placed = (
        P("sample", None),
        P(("prefix", "sample"), None, None),
        P(("prefix", "sample"), None, None),
        P(("prefix", "sample")),
        P("sample", "prefix", None),
        P("sample", "prefix", None),
        P("sample"),
    )
    return jax.shard_map(
        body, mesh=mesh, in_specs=placed, out_specs=P("sample", "prefix"), check_vma=False
    )
```

time: 544 us -> 100 us (0.18)
  the two profiles are of different devices: /device:TPU:1 before, /device:TPU:32 now
where the time goes in v1:
time: 100 us; the launch traced here: 99.7 us
  blocking collectives  84.3 us (84%)
  Pallas kernels  7.5 us (8%)
  local copies, waits for them, and re-layouts  5.86 us (6%)
  starting transfers between devices  1.92 us (2%)
    all_to_all x1, blocking collectives, body(): every_query = lax.all_to_all(query_blocks, 'sample', 0, 0)  44.9 us
    all_to_all x1, blocking collectives, body(): summed = lax.all_to_all(summed, 'sample', 0, 0)  22.1 us
    all_to_all x1, blocking collectives, body(): lax.all_to_all(partial, 'prefix', 0, 0, axis_index_groups=same_core)  17.3 us
    unnamed x24, local copies, waits for them, and re-layouts  5.86 us
    pallas_call x1, Pallas kernels, body(): pl.pallas_call(attend_kernel, out_shape=jax.ShapeDtypeStruct((PLANE, BLOC...  5.17 us
  transfers between devices with their start and end apart: 1, of which 0 were waited for; matrix products, arithmetic and copies ran while one was open for 0% of the time, Pallas kernels for 0%

profile of v1, /device:TPU:32, one launch (start us, length us, event | category | flops | bytes accessed | tf_op | source)
XLA Modules:
  0.0 99.7 jit_solution(3033877584311599780)
XLA Ops:
  0.0 1.2 %copy-done = bf16[4,128,1024]{2,1,0:T(8,128)(2,1)S(1)} copy-done((bf16[4,128,1024]{2,1,0:T(8,128)(2,1)S(1)}, bf16[4,128,1024]{2,1,0:T(8,128)(2,1)}, u32[]{:S(2)}) %copy-start) | copy-done | bytes 1048600
  1.2 0.0 copy-start.2
  1.2 1.2 %copy-done.2 = bf16[4,128,1024]{2,1,0:T(8,128)(2,1)S(1)} copy-done((bf16[4,128,1024]{2,1,0:T(8,128)(2,1)S(1)}, bf16[4,128,1024]{2,1,0:T(8,128)(2,1)}, u32[]{:S(2)}) %copy-start.2) | copy-done | bytes 1048600
  2.5 0.0 copy-start.4
  2.5 0.9 copy-done.4
  3.4 0.0 copy-start.6
  3.4 0.9 copy-done.6
  4.4 0.0 copy-start.8
  4.4 0.8 copy-done.8
  5.2 0.0 copy-start.9
  5.2 0.7 copy-done.9
  5.8 0.0 copy-start.1
  5.8 0.0 copy-start.3
  5.9 0.0 copy-start.5
  5.9 0.0 copy-start.7
  5.9 0.0 copy-start.10
  5.9 0.0 copy-start.11
  5.9 0.8 stage.1
  6.7 1.9 %collective-permute-start = (bf16[4,336,1024]{2,1,0:T(8,128)(2,1)S(1)}, bf16[4,336,1024]{2,1,0:T(8,128)(2,1)S(1)}, u32[]{:S(2)}, u32[]{:S(2)}) collective-permute-start(bf16[4,336,1024]{2,1,0:T(8,128)(2,1)S(1)} %get-tuple-element.8), channel_id=1, source_target_pairs={{0,16},{16,0},{32,48},{48,32},{64,80},{80,64},{96,112},{112,96},{1... | collective-permute-start | bytes 8257544 | tf_op jit(solution)/shard_map/ppermute | solution.py:243
  8.7 44.9 %all_to_all.15.queries_hbm = bf16[16,128,128]{2,1,0:T(8,128)(2,1)S(1)} all-to-all(bf16[16,128,128]{2,1,0:T(8,128)(2,1)S(1)} %get-tuple-element.7), channel_id=1, replica_groups=mesh['prefix'=32,'sample'=16] {'sample'}, dimensions={0} | all-to-all | bytes 1048576 | tf_op jit(solution)/shard_map/all_to_all | solution.py:244
  53.5 0.0 collective-permute-done.got_hbm
  53.5 0.0 copy-done.1
  53.5 0.0 copy-done.3
  53.5 0.0 copy-done.5
  53.5 0.0 copy-done.7
  53.6 0.0 copy-done.10
  53.6 0.0 copy-done.11
  53.6 5.2 %attend.1 = bf16[16,160,128]{2,1,0:T(8,128)(2,1)S(1)} custom-call(s32[4]{0:T(128)S(1)} %copy-done.10, s32[4]{0:T(128)S(1)} %copy-done.11, bf16[16,128,128]{2,1,0:T(8,128)(2,1)S(1)} %all_to_all.15.queries_hbm, bf16[4,128,1024]{2,1,0:T(8,128)(2,1)S(1)} %copy-done.1, bf16[4,128,1024]{2,1,0:T(8,128)(2,1)S(1)} %copy-done.3, bf16[4,32,1024]{2,1,0:T(8,128)(2,1)S(1)} %copy-done.5, ...), custom_call_target="tpu_custom_call" | custom-call | tf_op jit(solution)/shard_map/attend/pallas_call | solution.py:245
  58.8 17.3 %all_to_all.16.got = bf16[16,160,128]{2,1,0:T(8,128)(2,1)S(1)} all-to-all(bf16[16,160,128]{2,1,0:T(8,128)(2,1)S(1)} %attend.1), channel_id=1, replica_groups={{0,32,64,96,128,160,192,224,256,288,320,352,384,416,448,480},{16,48,80,..., dimensions={0} | all-to-all | bytes 1310720 | tf_op jit(solution)/shard_map/all_to_all | solution.py:269
  76.1 0.7 plane.1
  76.8 22.1 %all_to_all.17.got = f32[16,16,128]{2,1,0:T(8,128)S(1)} all-to-all(f32[16,16,128]{2,1,0:T(8,128)S(1)} %plane.1), channel_id=1, replica_groups=mesh['prefix'=32,'sample'=16] {'sample'}, dimensions={0} | all-to-all | bytes 262144 | tf_op jit(solution)/shard_map/all_to_all | solution.py:278
  99.0 0.7 final.1
  (1 shorter events, 0.0 us)
Async XLA Ops:
  0.0 1.2 %copy-start = (bf16[4,128,1024]{2,1,0:T(8,128)(2,1)S(1)}, bf16[4,128,1024]{2,1,0:T(8,128)(2,1)}, u32[]{:S(2)}) copy-start(bf16[4,128,1024]{2,1,0:T(8,128)(2,1)} %keys_hbm.1) | copy-start | bytes 3145732
  1.2 1.2 %copy-start.2 = (bf16[4,128,1024]{2,1,0:T(8,128)(2,1)S(1)}, bf16[4,128,1024]{2,1,0:T(8,128)(2,1)}, u32[]{:S(2)}) copy-start(bf16[4,128,1024]{2,1,0:T(8,128)(2,1)} %values_hbm.1) | copy-start | bytes 3145732
  2.5 0.9 copy-start.4
  3.4 0.9 copy-start.6
  4.4 0.8 copy-start.8
  5.2 0.7 copy-start.9
  5.8 47.7 %copy-start.1 = (bf16[4,128,1024]{2,1,0:T(8,128)(2,1)S(1)}, bf16[4,128,1024]{2,1,0:T(8,128)(2,1)}, u32[]{:S(2)}) copy-start(bf16[4,128,1024]{2,1,0:T(8,128)(2,1)} %keys_hbm.1) | copy-start | bytes 3145732
  5.8 47.7 %copy-start.3 = (bf16[4,128,1024]{2,1,0:T(8,128)(2,1)S(1)}, bf16[4,128,1024]{2,1,0:T(8,128)(2,1)}, u32[]{:S(2)}) copy-start(bf16[4,128,1024]{2,1,0:T(8,128)(2,1)} %values_hbm.1) | copy-start | bytes 3145732
  5.9 47.7 %copy-start.5 = (bf16[4,32,1024]{2,1,0:T(8,128)(2,1)S(1)}, bf16[4,32,1024]{2,1,0:T(8,128)(2,1)}, u32[]{:S(2)}) copy-start(bf16[4,32,1024]{2,1,0:T(8,128)(2,1)} %suffix_keys_hbm.1) | copy-start | bytes 786436
  5.9 47.7 %copy-start.7 = (bf16[4,32,1024]{2,1,0:T(8,128)(2,1)S(1)}, bf16[4,32,1024]{2,1,0:T(8,128)(2,1)}, u32[]{:S(2)}) copy-start(bf16[4,32,1024]{2,1,0:T(8,128)(2,1)} %suffix_values_hbm.1) | copy-start | bytes 786436
  5.9 47.7 %copy-start.10 = (s32[4]{0:T(128)S(1)}, s32[4]{0:T(128)}, u32[]{:S(2)}) copy-start(s32[4]{0:T(128)} %page_prompt.3) | copy-start | bytes 52
  5.9 47.7 %copy-start.11 = (s32[4]{0:T(128)S(1)}, s32[4]{0:T(128)}, u32[]{:S(2)}) copy-start(s32[4]{0:T(128)} %suffix_len.1) | copy-start | bytes 52
  6.7 46.8 %collective-permute-start = (bf16[4,336,1024]{2,1,0:T(8,128)(2,1)S(1)}, bf16[4,336,1024]{2,1,0:T(8,128)(2,1)S(1)}, u32[]{:S(2)}, u32[]{:S(2)}) collective-permute-start(bf16[4,336,1024]{2,1,0:T(8,128)(2,1)S(1)} %get-tuple-element.8), channel_id=1, source_target_pairs={{0,16},{16,0},{32,48},{48,32},{64,80},{80,64},{96,112},{112,96},{1... | collective-permute-start | bytes 8257544 | tf_op jit(solution)/shard_map/ppermute | solution.py:243

commit v2 on v1

v2 whole, which is shorter than its diff:
```python
import math

import jax
import jax.numpy as jnp
from jax import lax
from jax.experimental import pallas as pl
from jax.experimental.pallas import tpu as pltpu
from jax.sharding import PartitionSpec as P

H = 64
KVH = 8
HD = 128
PAGE = 128
SPP = 16
PROMPTS = 4
CORES = 2
OWN = 4
SPAN = 32
PLANE = 16
DEPTH = 16
ROWS = 128
HEAD_ROWS = 64
STAT_ROWS = 32
BLOCK_ROWS = ROWS + STAT_ROWS
KEY_ROW = 0
VALUE_ROW = PAGE
SUFFIX_KEY_ROW = 2 * PAGE
SUFFIX_VALUE_ROW = 2 * PAGE + SPAN
MARK_ROW = 2 * PAGE + 2 * SPAN
SEND_ROWS = MARK_ROW + 16
NEG = -1e30
MIB = 1 << 20
SCALE = math.log2(math.e) / math.sqrt(HD)
F32 = jnp.float32
BF16 = jnp.bfloat16


def query_kernel(queries, out):
    core = lax.rem(lax.axis_index("prefix"), CORES)
    for a in range(KVH):
        parts = []
        for half in range(2):
            for mate in range(2):
                head = a * 8 + half * 4 + mate
                column = pl.multiple_of(head * HD + core * (2 * HD), HD)
                parts.append(queries[:, pl.ds(column, HD)].astype(F32))
        out[pl.ds(a * 16, 16), :] = jnp.concatenate(parts, axis=0).astype(BF16)


def copy_kernel(shifted, out):
    rows = shifted[...]
    for chip in range(PLANE):
        out[chip] = rows


def stage_kernel(page_prompt, pool_keys, pool_values, suffix_keys, suffix_values, out,
                 prompts, sems):
    pieces = ((pool_keys, KEY_ROW, PAGE), (pool_values, VALUE_ROW, PAGE),
              (suffix_keys, SUFFIX_KEY_ROW, SPAN), (suffix_values, SUFFIX_VALUE_ROW, SPAN))
    copies = [
        pltpu.make_async_copy(src, out.at[:, pl.ds(start, rows), :], sems.at[i])
        for i, (src, start, rows) in enumerate(pieces)
    ]
    prompt_copy = pltpu.make_async_copy(page_prompt, prompts, sems.at[4])
    prompt_copy.start()
    for copy in copies:
        copy.start()
    prompt_copy.wait()
    for slot in range(OWN):
        mark = jnp.full((16, KVH * HD), prompts[slot], jnp.int32)
        out[slot, pl.ds(MARK_ROW, 16), :] = mark.astype(F32).astype(BF16)
    for copy in copies:
        copy.wait()


def attend_kernel(page_prompt, suffix_len, queries, held, got, out,
                  scores, top, peak, total, acc):
    prefix = lax.axis_index("prefix")
    plane = lax.axis_index("sample")
    top[...] = jnp.full(top.shape, NEG, F32)
    total[...] = jnp.zeros(total.shape, F32)
    acc[...] = jnp.zeros(acc.shape, F32)

    prompts = [page_prompt[slot] for slot in range(OWN)]
    for slot in range(OWN):
        mark = got[slot, pl.ds(MARK_ROW, 16), pl.ds(0, HD)].astype(F32)
        prompts.append(jnp.max(mark).astype(jnp.int32))
    held_prompts = [jnp.maximum(prompt, 0) for prompt in prompts]

    own_prompt = lax.div(plane, 4)
    quarter = lax.rem(plane, 4)
    row = lax.broadcasted_iota(jnp.int32, (HEAD_ROWS, PAGE), 0)
    token = lax.broadcasted_iota(jnp.int32, (HEAD_ROWS, PAGE), 1)
    token_sample = token >> 5
    length = jnp.where(
        token_sample == 0, suffix_len[0],
        jnp.where(token_sample == 1, suffix_len[1],
                  jnp.where(token_sample == 2, suffix_len[2], suffix_len[3])))
    mine = ((row >> 4) == quarter) & ((row & 3) == token_sample)

    def live(part):
        owner = prefix if part == 0 else prefix + 1 - 2 * lax.rem(prefix, CORES)
        return mine & (owner * SPAN + (token & (SPAN - 1)) < length)

    def query_rows(prompt, a):
        return jnp.concatenate(
            [queries[(plane - prompt * 4 - q) & (DEPTH - 1), pl.ds(a * 16, 16), :]
             for q in range(4)], axis=0)

    def dot_keys(prompt, a, key):
        return SCALE * lax.dot_general(
            query_rows(prompt, a), key, (((1,), (1,)), ((), ())), preferred_element_type=F32)

    for part, pages in enumerate((held, got)):
        for slot in range(part * OWN, (part + 1) * OWN):
            for a in range(KVH):
                key = pages[slot % OWN, pl.ds(KEY_ROW, PAGE), pl.ds(a * HD, HD)]
                s = dot_keys(held_prompts[slot], a, key)
                s = jnp.where(prompts[slot] >= 0, s, NEG)
                scores[slot, a] = s
                top[held_prompts[slot], a] = jnp.maximum(top[held_prompts[slot], a], s)

    for part, pages in enumerate((held, got)):
        mask = live(part)
        for a in range(KVH):
            key = pages[:, pl.ds(SUFFIX_KEY_ROW, SPAN), pl.ds(a * HD, HD)]
            key = key.reshape(OWN * SPAN, HD)
            s = jnp.where(mask, dot_keys(own_prompt, a, key), NEG)
            scores[2 * OWN + part, a] = s
            top[own_prompt, a] = jnp.maximum(top[own_prompt, a], s)

    @pl.loop(0, PROMPTS)
    def _(prompt):
        for a in range(KVH):
            best = jnp.max(top[prompt, a], axis=1, keepdims=True)
            best = best.astype(BF16).astype(F32)
            peak[prompt, a] = jnp.broadcast_to(best, (HEAD_ROWS, HD))

    for part, pages in enumerate((held, got)):
        for slot in range(part * OWN, (part + 1) * OWN):
            prompt = held_prompts[slot]
            for a in range(KVH):
                value = pages[slot % OWN, pl.ds(VALUE_ROW, PAGE), pl.ds(a * HD, HD)]
                w = jnp.exp2(scores[slot, a] - peak[prompt, a])
                w = jnp.where(prompts[slot] >= 0, w, 0.0)
                total[prompt, a] += w
                acc[prompt, a] += jnp.dot(w.astype(BF16), value, preferred_element_type=F32)

    for part, pages in enumerate((held, got)):
        mask = live(part)
        for a in range(KVH):
            value = pages[:, pl.ds(SUFFIX_VALUE_ROW, SPAN), pl.ds(a * HD, HD)]
            value = value.reshape(OWN * SPAN, HD)
            w = jnp.where(mask, jnp.exp2(scores[2 * OWN + part, a] - peak[own_prompt, a]), 0.0)
            total[own_prompt, a] += w
            acc[own_prompt, a] += jnp.dot(w.astype(BF16), value, preferred_element_type=F32)

    lane = lax.broadcasted_iota(jnp.int32, (HEAD_ROWS, HD), 1)

    @pl.loop(0, KVH)
    def _(a):
        stats = jnp.zeros((HEAD_ROWS, HD), F32)
        for prompt in range(PROMPTS):
            low = jnp.sum(total[prompt, a], axis=1, keepdims=True)
            high = low.astype(BF16).astype(F32)
            stats = jnp.where(lane == prompt, peak[prompt, a], stats)
            stats = jnp.where(lane == 4 + prompt, high, stats)
            stats = jnp.where(lane == 8 + prompt, low - high, stats)
        for half in range(2):
            def pick(tile):
                return jnp.concatenate(
                    [tile[q * 16 + half * 8:q * 16 + half * 8 + 8] for q in range(4)], axis=0)
            for prompt in range(PROMPTS):
                out[a * 2 + half, pl.ds(prompt * 32, 32), :] = pick(acc[prompt, a]).astype(BF16)
            out[a * 2 + half, pl.ds(ROWS, STAT_ROWS), :] = pick(stats).astype(BF16)


def plane_kernel(got, out):
    best = jnp.full((STAT_ROWS, HD), NEG, F32)
    for src in range(PLANE):
        best = jnp.maximum(best, got[src, pl.ds(ROWS, STAT_ROWS), :].astype(F32))
    denominator = jnp.zeros((STAT_ROWS, HD), F32)
    sums = [jnp.zeros((STAT_ROWS, HD), F32) for _ in range(PROMPTS)]
    for src in range(PLANE):
        stats = got[src, pl.ds(ROWS, STAT_ROWS), :].astype(F32)
        weight = jnp.exp2(jnp.minimum(stats - best, 0.0))
        part = pltpu.roll(stats, HD - 4, 1) + pltpu.roll(stats, HD - 8, 1)
        denominator = denominator + weight * part
        for prompt in range(PROMPTS):
            tile = got[src, pl.ds(prompt * 32, 32), :].astype(F32)
            sums[prompt] = sums[prompt] + tile * weight[:, prompt:prompt + 1]
    lane = lax.broadcasted_iota(jnp.int32, (8, HD), 1)
    for prompt in range(PROMPTS):
        for quarter in range(4):
            rows = slice(quarter * 8, quarter * 8 + 8)
            stat = jnp.where(lane == 0, best[rows, prompt:prompt + 1],
                             denominator[rows, prompt:prompt + 1])
            out[prompt * 4 + quarter, pl.ds(0, 8), :] = sums[prompt][rows]
            out[prompt * 4 + quarter, pl.ds(8, 8), :] = stat


def final_kernel(got, out):
    best = got[0, pl.ds(8, 8), :]
    for src in range(1, DEPTH):
        best = jnp.maximum(best, got[src, pl.ds(8, 8), :])
    best = best[:, 0:1]
    denominator = jnp.zeros((8, 1), F32)
    numerator = jnp.zeros((8, HD), F32)
    for src in range(DEPTH):
        stat = got[src, pl.ds(8, 8), :]
        weight = jnp.exp2(stat[:, 0:1] - best)
        denominator = denominator + weight * stat[:, 1:2]
        numerator = numerator + weight * got[src, pl.ds(0, 8), :]
    mixed = (numerator / denominator).astype(BF16)
    out[...] = jnp.concatenate([mixed[0:4], mixed[4:8]], axis=1)


SMEM = pl.BlockSpec(memory_space=pltpu.SMEM)
VMEM = pl.BlockSpec(memory_space=pltpu.VMEM)
ANY = pl.BlockSpec(memory_space=pl.ANY)


def budget(mib):
    return pltpu.CompilerParams(vmem_limit_bytes=int(mib * MIB))


def body(queries, pool_keys, pool_values, page_prompt, suffix_keys, suffix_values, suffix_len):
    own_queries = pl.pallas_call(
        query_kernel,
        out_shape=jax.ShapeDtypeStruct((ROWS, HD), BF16),
        in_specs=[VMEM],
        out_specs=VMEM,
        compiler_params=budget(2),
        name="query",
    )(queries)
    held = pl.pallas_call(
        stage_kernel,
        out_shape=jax.ShapeDtypeStruct((OWN, SEND_ROWS, KVH * HD), BF16),
        in_specs=[ANY] * 5,
        out_specs=VMEM,
        scratch_shapes=[pltpu.SMEM((OWN,), jnp.int32), pltpu.SemaphoreType.DMA((5,))],
        compiler_params=budget(4),
        name="stage",
    )(*(pltpu.with_memory_space_constraint(array, pltpu.HBM)
        for array in (page_prompt, pool_keys, pool_values, suffix_keys, suffix_values)))
    shifted = lax.ppermute(
        own_queries, ("prefix", "sample"),
        [((chip * CORES + core) * DEPTH + z, (chip * CORES + core) * DEPTH + (z + chip) % DEPTH)
         for chip in range(PLANE) for core in range(CORES) for z in range(DEPTH)])
    got = lax.ppermute(held, "prefix", [(i, i ^ 1) for i in range(CORES * PLANE)])
    same_core = [[chip * CORES + core for chip in range(PLANE)] for core in range(CORES)]
    copies = pl.pallas_call(
        copy_kernel,
        out_shape=jax.ShapeDtypeStruct((PLANE, ROWS, HD), BF16),
        in_specs=[VMEM],
        out_specs=VMEM,
        compiler_params=budget(2),
        cost_estimate=pl.CostEstimate(flops=10**11, transcendentals=0, bytes_accessed=MIB),
        name="copies",
    )(shifted)
    every_query = lax.all_to_all(copies, "prefix", 0, 0, axis_index_groups=same_core)
    partial = pl.pallas_call(
        attend_kernel,
        out_shape=jax.ShapeDtypeStruct((PLANE, BLOCK_ROWS, HD), BF16),
        in_specs=[SMEM, SMEM, VMEM, VMEM, VMEM],
        out_specs=VMEM,
        scratch_shapes=[
            pltpu.VMEM((2 * OWN + 2, KVH, HEAD_ROWS, PAGE), F32),
            pltpu.VMEM((PROMPTS, KVH, HEAD_ROWS, PAGE), F32),
            pltpu.VMEM((PROMPTS, KVH, HEAD_ROWS, HD), F32),
            pltpu.VMEM((PROMPTS, KVH, HEAD_ROWS, PAGE), F32),
            pltpu.VMEM((PROMPTS, KVH, HEAD_ROWS, HD), F32),
        ],
        compiler_params=budget(18),
        name="attend",
    )(page_prompt, suffix_len, every_query, held, got)
    partial = lax.all_to_all(partial, "prefix", 0, 0, axis_index_groups=same_core)
    summed = pl.pallas_call(
        plane_kernel,
        out_shape=jax.ShapeDtypeStruct((DEPTH, 16, HD), F32),
        in_specs=[VMEM],
        out_specs=VMEM,
        compiler_params=budget(4),
        name="plane",
    )(partial)
    summed = lax.all_to_all(summed, "sample", 0, 0)
    return pl.pallas_call(
        final_kernel,
        out_shape=jax.ShapeDtypeStruct((OWN, 2 * HD), BF16),
        in_specs=[VMEM],
        out_specs=VMEM,
        compiler_params=budget(2),
        name="final",
    )(summed)


def solution(mesh):
    placed = (
        P("sample", None),
        P(("prefix", "sample"), None, None),
        P(("prefix", "sample"), None, None),
        P(("prefix", "sample")),
        P("sample", "prefix", None),
        P("sample", "prefix", None),
        P("sample"),
    )
    return jax.shard_map(
        body, mesh=mesh, in_specs=placed, out_specs=P("sample", "prefix"), check_vma=False
    )
```

time: 100 us -> 82.4 us (0.82)
  the two profiles are of different devices: /device:TPU:32 before, /device:TPU:2 now
where the time goes in v2:
time: 82.4 us; the launch traced here: 82 us
  blocking collectives  59.5 us (72%)
  starting transfers between devices  11 us (13%)
  Pallas kernels  8.66 us (11%)
  waiting for transfers between devices  1.89 us (2%)
  local copies, waits for them, and re-layouts  0.85 us (1%)
    all_to_all x1, blocking collectives, body(): summed = lax.all_to_all(summed, 'sample', 0, 0)  22.1 us
    all_to_all x1, blocking collectives, body(): lax.all_to_all(copies, 'prefix', 0, 0, axis_index_groups=same_core)  21 us
    all_to_all x1, blocking collectives, body(): lax.all_to_all(partial, 'prefix', 0, 0, axis_index_groups=same_core)  16.4 us
    ppermute x1, starting transfers between devices, body(): lax.ppermute(own_queries, ('prefix', 'sample'), [((chip * CORES + core) *...  9.1 us
    pallas_call x1, Pallas kernels, body(): pl.pallas_call(attend_kernel, out_shape=jax.ShapeDtypeStruct((PLANE, BLOC...  5.33 us
    ppermute x1, starting transfers between devices, body(): lax.ppermute(held, 'prefix', [(i, i ^ 1) for i in range(CORES * PLANE)])  1.92 us
    ppermute x1, waiting for transfers between devices, body(): lax.ppermute(own_queries, ('prefix', 'sample'), [((chip * CORES + core) *...  1.89 us
    pallas_call x1, Pallas kernels, body(): pl.pallas_call(stage_kernel, out_shape=jax.ShapeDtypeStruct((OWN, SEND_RO...  1.71 us
  transfers between devices with their start and end apart: 2, of which 1 were waited for; matrix products, arithmetic and copies ran while one was open for 0% of the time, Pallas kernels for 2%

profile of v2, /device:TPU:2, one launch (start us, length us, event | category | flops | bytes accessed | tf_op | source)
XLA Modules:
  0.0 82.0 jit_solution(11681565442456435416)
XLA Ops:
  0.0 0.0 copy-start
  0.0 0.8 %copy-done = bf16[4,8192]{1,0:T(4,128)(2,1)S(1)} copy-done((bf16[4,8192]{1,0:T(4,128)(2,1)S(1)}, bf16[4,8192]{1,0:T(4,128)(2,1)}, u32[]{:S(2)}) %copy-start) | copy-done | bytes 65560
  0.9 9.1 %collective-permute-start = (bf16[128,128]{1,0:T(8,128)(2,1)S(1)}, bf16[128,128]{1,0:T(8,128)(2,1)S(1)}, u32[]{:S(2)}, u32[]{:S(2)}) collective-permute-start(bf16[128,128]{1,0:T(8,128)(2,1)S(1)} %query.1), channel_id=1, source_target_pairs={{0,0},{1,1},{2,2},{3,3},{4,4},{5,5},{6,6},{7,7},{8,8},{9,9},{10,10... | collective-permute-start | bytes 98312 | tf_op jit(solution)/shard_map/ppermute | solution.py:246
  10.0 1.7 %stage.1.held = bf16[4,336,1024]{2,1,0:T(8,128)(2,1)S(1)} custom-call(s32[4]{0:T(128)} %page_prompt.3, bf16[4,128,1024]{2,1,0:T(8,128)(2,1)} %pool_keys.1, bf16[4,128,1024]{2,1,0:T(8,128)(2,1)} %pool_values.1, bf16[4,32,1024]{2,1,0:T(8,128)(2,1)} %suffix_keys.1, bf16[4,32,1024]{2,1,0:T(8,128)(2,1)} %suffix_values.1), custom_call_target="tpu_custom_call" | custom-call | tf_op jit(solution)/shard_map/stage/pallas_call | solution.py:236
  11.7 0.0 copy-start.1
  11.7 0.0 copy-start.2
  11.7 1.9 %collective-permute-start.1 = (bf16[4,336,1024]{2,1,0:T(8,128)(2,1)S(1)}, bf16[4,336,1024]{2,1,0:T(8,128)(2,1)S(1)}, u32[]{:S(2)}, u32[]{:S(2)}) collective-permute-start(bf16[4,336,1024]{2,1,0:T(8,128)(2,1)S(1)} %stage.1.held), channel_id=1, source_target_pairs={{0,16},{16,0},{32,48},{48,32},{64,80},{80,64},{96,112},{112,96},{1... | collective-permute-start | bytes 8257544 | tf_op jit(solution)/shard_map/ppermute | solution.py:250
  13.7 1.9 %collective-permute-done.shifted = bf16[128,128]{1,0:T(8,128)(2,1)S(1)} collective-permute-done((bf16[128,128]{1,0:T(8,128)(2,1)S(1)}, bf16[128,128]{1,0:T(8,128)(2,1)S(1)}, u32[]{:S(2)}, u32[]{:S(2)}) %collective-permute-start) | collective-permute-done | bytes 32800 | tf_op jit(solution)/shard_map/ppermute | solution.py:246
  15.5 0.1 copies.1
  15.6 21.0 %all_to_all.15.queries = bf16[16,128,128]{2,1,0:T(8,128)(2,1)S(1)} all-to-all(bf16[16,128,128]{2,1,0:T(8,128)(2,1)S(1)} %copies.1), channel_id=1, replica_groups={{0,32,64,96,128,160,192,224,256,288,320,352,384,416,448,480},{16,48,80,..., dimensions={0} | all-to-all | bytes 1048576 | tf_op jit(solution)/shard_map/all_to_all | solution.py:261
  36.7 0.0 collective-permute-done.1.got
  36.7 0.0 copy-done.1
  36.7 0.0 copy-done.2
  36.7 5.3 %attend.1 = bf16[16,160,128]{2,1,0:T(8,128)(2,1)S(1)} custom-call(s32[4]{0:T(128)S(1)} %copy-done.1, s32[4]{0:T(128)S(1)} %copy-done.2, bf16[16,128,128]{2,1,0:T(8,128)(2,1)S(1)} %all_to_all.15.queries, bf16[4,336,1024]{2,1,0:T(8,128)(2,1)S(1)} %stage.1.held, bf16[4,336,1024]{2,1,0:T(8,128)(2,1)S(1)} %collective-permute-done.1.got), custom_call_target="tpu_custom_call" | custom-call | tf_op jit(solution)/shard_map/attend/pallas_call | solution.py:262
  42.0 16.4 %all_to_all.16.got = bf16[16,160,128]{2,1,0:T(8,128)(2,1)S(1)} all-to-all(bf16[16,160,128]{2,1,0:T(8,128)(2,1)S(1)} %attend.1), channel_id=1, replica_groups={{0,32,64,96,128,160,192,224,256,288,320,352,384,416,448,480},{16,48,80,..., dimensions={0} | all-to-all | bytes 1310720 | tf_op jit(solution)/shard_map/all_to_all | solution.py:277
  58.4 0.7 plane.1
  59.1 22.1 %all_to_all.17.got = f32[16,16,128]{2,1,0:T(8,128)S(1)} all-to-all(f32[16,16,128]{2,1,0:T(8,128)S(1)} %plane.1), channel_id=1, replica_groups=mesh['prefix'=32,'sample'=16] {'sample'}, dimensions={0} | all-to-all | bytes 262144 | tf_op jit(solution)/shard_map/all_to_all | solution.py:286
  81.2 0.7 final.1
  (1 shorter events, 0.0 us)
Async XLA Ops:
  0.0 0.8 %copy-start = (bf16[4,8192]{1,0:T(4,128)(2,1)S(1)}, bf16[4,8192]{1,0:T(4,128)(2,1)}, u32[]{:S(2)}) copy-start(bf16[4,8192]{1,0:T(4,128)(2,1)} %queries.1) | copy-start | bytes 196612
  0.9 14.7 %collective-permute-start = (bf16[128,128]{1,0:T(8,128)(2,1)S(1)}, bf16[128,128]{1,0:T(8,128)(2,1)S(1)}, u32[]{:S(2)}, u32[]{:S(2)}) collective-permute-start(bf16[128,128]{1,0:T(8,128)(2,1)S(1)} %query.1), channel_id=1, source_target_pairs={{0,0},{1,1},{2,2},{3,3},{4,4},{5,5},{6,6},{7,7},{8,8},{9,9},{10,10... | collective-permute-start | bytes 98312 | tf_op jit(solution)/shard_map/ppermute | solution.py:246
  11.7 25.0 %copy-start.1 = (s32[4]{0:T(128)S(1)}, s32[4]{0:T(128)}, u32[]{:S(2)}) copy-start(s32[4]{0:T(128)} %page_prompt.3) | copy-start | bytes 52
  11.7 25.0 %copy-start.2 = (s32[4]{0:T(128)S(1)}, s32[4]{0:T(128)}, u32[]{:S(2)}) copy-start(s32[4]{0:T(128)} %suffix_len.1) | copy-start | bytes 52
  11.7 24.9 %collective-permute-start.1 = (bf16[4,336,1024]{2,1,0:T(8,128)(2,1)S(1)}, bf16[4,336,1024]{2,1,0:T(8,128)(2,1)S(1)}, u32[]{:S(2)}, u32[]{:S(2)}) collective-permute-start(bf16[4,336,1024]{2,1,0:T(8,128)(2,1)S(1)} %stage.1.held), channel_id=1, source_target_pairs={{0,16},{16,0},{32,48},{48,32},{64,80},{80,64},{96,112},{112,96},{1... | collective-permute-start | bytes 8257544 | tf_op jit(solution)/shard_map/ppermute | solution.py:250

commit v3 on v2

v3 whole, which is shorter than its diff:
```python
import math

import jax
import jax.numpy as jnp
from jax import lax
from jax.experimental import pallas as pl
from jax.experimental.pallas import tpu as pltpu
from jax.sharding import PartitionSpec as P

H = 64
KVH = 8
HD = 128
PAGE = 128
SPP = 16
PROMPTS = 4
CORES = 2
OWN = 4
SPAN = 32
PLANE = 16
DEPTH = 16
ROWS = 128
HEAD_ROWS = 64
STAT_ROWS = 16
BLOCK_ROWS = ROWS + STAT_ROWS
KEY_ROW = 0
VALUE_ROW = PAGE
SUFFIX_KEY_ROW = 2 * PAGE
SUFFIX_VALUE_ROW = 2 * PAGE + SPAN
MARK_ROW = 2 * PAGE + 2 * SPAN
SEND_ROWS = MARK_ROW + 16
NEG = -1e30
MIB = 1 << 20
SCALE = math.log2(math.e) / math.sqrt(HD)
CHIP_ORDER = (0, 4, 1, 2, 8, 3, 12, 5, 6, 9, 13, 7, 14, 11, 10, 15)
DISTANCES = (8, 7, 9, 6, 10, 5, 11, 4, 12, 3, 13, 2, 14, 1, 15, 0)
DISTANCE_OF = dict(zip(CHIP_ORDER, DISTANCES))
CHIP_OF = dict(zip(DISTANCES, CHIP_ORDER))
F32 = jnp.float32
BF16 = jnp.bfloat16


def query_kernel(queries, out):
    core = lax.rem(lax.axis_index("prefix"), CORES)
    for a in range(KVH):
        parts = []
        for half in range(2):
            for mate in range(2):
                head = a * 8 + half * 4 + mate
                column = pl.multiple_of(head * HD + core * (2 * HD), HD)
                parts.append(queries[:, pl.ds(column, HD)].astype(F32))
        out[pl.ds(a * 16, 16), :] = jnp.concatenate(parts, axis=0).astype(BF16)


def copy_kernel(shifted, out):
    rows = shifted[...]
    for chip in range(PLANE):
        out[chip] = rows


def stage_kernel(page_prompt, pool_keys, pool_values, suffix_keys, suffix_values, out,
                 keys, suffix, prompts, sems):
    pieces = ((page_prompt, prompts), (pool_keys, keys), (suffix_keys, suffix),
              (pool_values, out.at[:, pl.ds(VALUE_ROW, PAGE), :]),
              (suffix_values, out.at[:, pl.ds(SUFFIX_VALUE_ROW, SPAN), :]))
    copies = [pltpu.make_async_copy(src, dst, sems.at[i]) for i, (src, dst) in enumerate(pieces)]
    for copy in copies:
        copy.start()
    copies[0].wait()
    for slot in range(OWN):
        mark = jnp.full((16, KVH * HD), prompts[slot], jnp.int32)
        out[slot, pl.ds(MARK_ROW, 16), :] = mark.astype(F32).astype(BF16)
    copies[1].wait()
    for slot in range(OWN):
        for a in range(KVH):
            head = pl.ds(a * HD, HD)
            out[slot, pl.ds(KEY_ROW, PAGE), head] = keys[slot, :, head].T
    copies[2].wait()
    for a in range(KVH):
        head = pl.ds(a * HD, HD)
        turned = suffix[:, :, head].reshape(OWN * SPAN, HD).T
        out[:, pl.ds(SUFFIX_KEY_ROW, SPAN), head] = turned.reshape(OWN, SPAN, OWN * SPAN)
    for copy in copies[3:]:
        copy.wait()


def attend_kernel(page_prompt, suffix_len, chip_of, queries, held, got, out, scores,
                  suffix_scores, *buffers):
    top, peak, total, acc = (buffers[i * KVH:(i + 1) * KVH] for i in range(4))
    prefix = lax.axis_index("prefix")
    plane = lax.axis_index("sample")
    sign = 1 - 2 * lax.rem(prefix, CORES)
    for a in range(KVH):
        top[a][...] = jnp.full(top[a].shape, NEG, F32)
        total[a][...] = jnp.zeros(total[a].shape, F32)
        acc[a][...] = jnp.zeros(acc[a].shape, F32)
        peak[a][PROMPTS] = jnp.zeros((HEAD_ROWS, HD), F32)

    prompts = [page_prompt[slot] for slot in range(OWN)]
    for slot in range(OWN):
        mark = got[slot, pl.ds(MARK_ROW, 16), pl.ds(0, HD)].astype(F32)
        prompts.append(jnp.max(mark).astype(jnp.int32))
    prompts = [jnp.where(prompt >= 0, prompt, PROMPTS) for prompt in prompts]

    own_prompt = lax.div(plane, 4)
    quarter = lax.rem(plane, 4)
    row = lax.broadcasted_iota(jnp.int32, (16, PAGE), 0)
    token = lax.broadcasted_iota(jnp.int32, (16, PAGE), 1)
    token_sample = token >> 5
    length = jnp.where(
        token_sample == 0, suffix_len[0],
        jnp.where(token_sample == 1, suffix_len[1],
                  jnp.where(token_sample == 2, suffix_len[2], suffix_len[3])))
    own_rows = pl.ds(pl.multiple_of(quarter * 16, 16), 16)

    def live(part):
        owner = prefix if part == 0 else prefix + sign
        position = owner * SPAN + (token & (SPAN - 1))
        return ((row & 3) == token_sample) & (position < length)

    def chip_rows(sample_plane, a):
        chip = chip_of[(sign * (plane - sample_plane)) & (DEPTH - 1)]
        return queries[chip, pl.ds(a * 16, 16), :]

    def query_rows(prompt, a):
        return jnp.concatenate([chip_rows(prompt * 4 + q, a) for q in range(4)], axis=0)

    def dot_keys(rows, key):
        return SCALE * lax.dot_general(
            rows, key, (((1,), (0,)), ((), ())), preferred_element_type=F32)

    for part, pages in enumerate((held, got)):
        for slot in range(part * OWN, (part + 1) * OWN):
            for a in range(KVH):
                key = pages[slot % OWN, pl.ds(KEY_ROW, PAGE), pl.ds(a * HD, HD)]
                s = dot_keys(query_rows(prompts[slot], a), key)
                scores[slot, a] = s
                top[a][prompts[slot]] = jnp.maximum(top[a][prompts[slot]], s)

    for part, pages in enumerate((held, got)):
        mask = live(part)
        for a in range(KVH):
            key = pages[:, pl.ds(SUFFIX_KEY_ROW, SPAN), pl.ds(a * HD, HD)]
            key = key.reshape(HD, OWN * SPAN)
            s = jnp.where(mask, dot_keys(chip_rows(plane, a), key), NEG)
            suffix_scores[part, a] = s
            top[a][own_prompt, own_rows] = jnp.maximum(top[a][own_prompt, own_rows], s)

    for a in range(KVH):
        for prompt in range(PROMPTS):
            best = jnp.max(top[a][prompt], axis=1, keepdims=True)
            best = best.astype(BF16).astype(F32)
            peak[a][prompt] = jnp.broadcast_to(best, (HEAD_ROWS, HD))

    for part, pages in enumerate((held, got)):
        for slot in range(part * OWN, (part + 1) * OWN):
            prompt = prompts[slot]
            for a in range(KVH):
                value = pages[slot % OWN, pl.ds(VALUE_ROW, PAGE), pl.ds(a * HD, HD)]
                w = jnp.exp2(scores[slot, a] - peak[a][prompt])
                total[a][prompt] += w
                acc[a][prompt] += jnp.dot(w.astype(BF16), value, preferred_element_type=F32)

    for part, pages in enumerate((held, got)):
        mask = live(part)
        for a in range(KVH):
            value = pages[:, pl.ds(SUFFIX_VALUE_ROW, SPAN), pl.ds(a * HD, HD)]
            value = value.reshape(OWN * SPAN, HD)
            w = jnp.exp2(suffix_scores[part, a] - peak[a][own_prompt, own_rows])
            w = jnp.where(mask, w, 0.0)
            total[a][own_prompt, own_rows] += w
            acc[a][own_prompt, own_rows] += jnp.dot(
                w.astype(BF16), value, preferred_element_type=F32)

    lane = lax.broadcasted_iota(jnp.int32, (HEAD_ROWS, HD), 1)

    for a in range(KVH):
        stats = jnp.zeros((HEAD_ROWS, HD), F32)
        for prompt in range(PROMPTS):
            low = jnp.sum(total[a][prompt], axis=1, keepdims=True)
            high = low.astype(BF16).astype(F32)
            stats = jnp.where(lane == prompt, peak[a][prompt], stats)
            stats = jnp.where(lane == 4 + prompt, high, stats)
            stats = jnp.where(lane == 8 + prompt, low - high, stats)
        for half in range(2):
            def quarter_rows(tile, q):
                return tile[q * 16 + half * 8:q * 16 + half * 8 + 8]
            for prompt in range(PROMPTS):
                sums = acc[a][prompt]
                rows = jnp.concatenate([quarter_rows(sums, q) for q in range(4)], axis=0)
                out[a * 2 + half, pl.ds(prompt * 32, 32), :] = rows.astype(BF16)
            packed = jnp.concatenate(
                [quarter_rows(stats, q) + pltpu.roll(quarter_rows(stats, q + 1), 16, 1)
                 for q in (0, 2)], axis=0)
            out[a * 2 + half, pl.ds(ROWS, STAT_ROWS), :] = packed.astype(BF16)


def plane_kernel(got, out):
    stats = [got[src, pl.ds(ROWS, STAT_ROWS), :].astype(F32) for src in range(PLANE)]
    best = stats[0]
    for src in range(1, PLANE):
        best = jnp.maximum(best, stats[src])
    denominator = jnp.zeros((STAT_ROWS, HD), F32)
    sums = [jnp.zeros((8, HD), F32) for _ in range(DEPTH)]

    def column(tile, prompt, quarter):
        rows, start = quarter // 2 * 8, quarter % 2 * 16 + prompt
        return tile[rows:rows + 8, start:start + 1]

    for src in range(PLANE):
        weight = jnp.exp2(jnp.minimum(stats[src] - best, 0.0))
        part = pltpu.roll(stats[src], HD - 4, 1) + pltpu.roll(stats[src], HD - 8, 1)
        denominator = denominator + weight * part
        for prompt in range(PROMPTS):
            tile = got[src, pl.ds(prompt * 32, 32), :].astype(F32)
            for quarter in range(4):
                i = prompt * 4 + quarter
                sums[i] = sums[i] + (
                    tile[quarter * 8:quarter * 8 + 8] * column(weight, prompt, quarter))
    high = denominator.astype(BF16).astype(F32)
    lane = lax.broadcasted_iota(jnp.int32, (8, HD), 1)
    for prompt in range(PROMPTS):
        for quarter in range(4):
            i = prompt * 4 + quarter
            stat = jnp.where(
                lane == 0, column(best, prompt, quarter),
                jnp.where(lane == 1, column(high, prompt, quarter),
                          column(denominator - high, prompt, quarter)))
            out[i] = jnp.concatenate([sums[i], stat], axis=0).astype(BF16)


def final_kernel(got, out):
    tiles = [got[src].astype(F32) for src in range(DEPTH)]
    best = tiles[0][8:16]
    for src in range(1, DEPTH):
        best = jnp.maximum(best, tiles[src][8:16])
    best = best[:, 0:1]
    denominator = jnp.zeros((8, 1), F32)
    numerator = jnp.zeros((8, HD), F32)
    for tile in tiles:
        stat = tile[8:16]
        weight = jnp.exp2(stat[:, 0:1] - best)
        denominator = denominator + weight * (stat[:, 1:2] + stat[:, 2:3])
        numerator = numerator + weight * tile[0:8]
    mixed = (numerator / denominator).astype(BF16)
    out[...] = jnp.concatenate([mixed[0:4], mixed[4:8]], axis=1)


SMEM = pl.BlockSpec(memory_space=pltpu.SMEM)
VMEM = pl.BlockSpec(memory_space=pltpu.VMEM)
ANY = pl.BlockSpec(memory_space=pl.ANY)


def budget(mib):
    return pltpu.CompilerParams(vmem_limit_bytes=int(mib * MIB))


def body(queries, pool_keys, pool_values, page_prompt, suffix_keys, suffix_values, suffix_len):
    own_queries = pl.pallas_call(
        query_kernel,
        out_shape=jax.ShapeDtypeStruct((ROWS, HD), BF16),
        in_specs=[VMEM],
        out_specs=VMEM,
        compiler_params=budget(2),
        name="query",
    )(queries)
    held = pl.pallas_call(
        stage_kernel,
        out_shape=jax.ShapeDtypeStruct((OWN, SEND_ROWS, KVH * HD), BF16),
        in_specs=[ANY] * 5,
        out_specs=VMEM,
        scratch_shapes=[
            pltpu.VMEM((OWN, PAGE, KVH * HD), BF16),
            pltpu.VMEM((OWN, SPAN, KVH * HD), BF16),
            pltpu.SMEM((OWN,), jnp.int32),
            pltpu.SemaphoreType.DMA((5,)),
        ],
        compiler_params=budget(6),
        name="stage",
    )(*(pltpu.with_memory_space_constraint(array, pltpu.HBM)
        for array in (page_prompt, pool_keys, pool_values, suffix_keys, suffix_values)))
    shifted = lax.ppermute(
        own_queries, ("prefix", "sample"),
        [((chip * CORES + core) * DEPTH + z, (chip * CORES + core) * DEPTH + (z + (1 - 2 * core) * DISTANCE_OF[chip]) % DEPTH)
         for chip in range(PLANE) for core in range(CORES) for z in range(DEPTH)])
    got = lax.ppermute(held, "prefix", [(i, i ^ 1) for i in range(CORES * PLANE)])
    same_core = [[chip * CORES + core for chip in range(PLANE)] for core in range(CORES)]
    copies = pl.pallas_call(
        copy_kernel,
        out_shape=jax.ShapeDtypeStruct((PLANE, ROWS, HD), BF16),
        in_specs=[VMEM],
        out_specs=VMEM,
        compiler_params=budget(2),
        cost_estimate=pl.CostEstimate(flops=10**11, transcendentals=0, bytes_accessed=MIB),
        name="copies",
    )(shifted)
    every_query = lax.all_to_all(copies, "prefix", 0, 0, axis_index_groups=same_core)
    chip_of = jnp.array([CHIP_OF[distance] for distance in range(DEPTH)], jnp.int32)
    partial = pl.pallas_call(
        attend_kernel,
        out_shape=jax.ShapeDtypeStruct((PLANE, BLOCK_ROWS, HD), BF16),
        in_specs=[SMEM, SMEM, SMEM, VMEM, VMEM, VMEM],
        out_specs=VMEM,
        scratch_shapes=[
            pltpu.VMEM((2 * OWN, KVH, HEAD_ROWS, PAGE), F32),
            pltpu.VMEM((2, KVH, 16, PAGE), F32),
        ] + [pltpu.VMEM((PROMPTS + 1, HEAD_ROWS, HD), F32)] * (4 * KVH),
        compiler_params=budget(18),
        name="attend",
    )(page_prompt, suffix_len, chip_of, every_query, held, got)
    partial = lax.all_to_all(partial, "prefix", 0, 0, axis_index_groups=same_core)
    summed = pl.pallas_call(
        plane_kernel,
        out_shape=jax.ShapeDtypeStruct((DEPTH, 16, HD), BF16),
        in_specs=[VMEM],
        out_specs=VMEM,
        compiler_params=budget(4),
        name="plane",
    )(partial)
    summed = lax.all_to_all(summed, "sample", 0, 0)
    return pl.pallas_call(
        final_kernel,
        out_shape=jax.ShapeDtypeStruct((OWN, 2 * HD), BF16),
        in_specs=[VMEM],
        out_specs=VMEM,
        compiler_params=budget(2),
        name="final",
    )(summed)


def solution(mesh):
    placed = (
        P("sample", None),
        P(("prefix", "sample"), None, None),
        P(("prefix", "sample"), None, None),
        P(("prefix", "sample")),
        P("sample", "prefix", None),
        P("sample", "prefix", None),
        P("sample"),
    )
    return jax.shard_map(
        body, mesh=mesh, in_specs=placed, out_specs=P("sample", "prefix"), check_vma=False
    )
```

time: 82.4 us -> 76 us (0.922)
  blocking collectives: 59.5 us -> 51 us
  starting transfers between devices: 11 us -> 16.9 us
  waiting for transfers between devices: 1.89 us -> 0.01 us
  Pallas kernels: 8.66 us -> 6.87 us
    all_to_all x1, blocking collectives: 21 us -> 14.5 us  [body(): lax.all_to_all(copies, 'prefix', 0, 0, axis_index_groups=same_core)]
    ppermute x1, starting transfers between devices: 9.1 us -> 13.2 us  [body(): lax.ppermute(own_queries, ('prefix', 'sample'), [((chip * CORES + core) *...]
    pallas_call x1, Pallas kernels: 5.33 us -> 3.43 us  [body(): pl.pallas_call(attend_kernel, out_shape=jax.ShapeDtypeStruct((PLANE, BLOC...]
    ppermute x1, waiting for transfers between devices: 1.89 us -> 0.01 us  [body(): lax.ppermute(own_queries, ('prefix', 'sample'), [((chip * CORES + core) *...]
    ppermute x1, starting transfers between devices: 1.92 us -> 3.71 us  [body(): lax.ppermute(held, 'prefix', [(i, i ^ 1) for i in range(CORES * PLANE)])]
    all_to_all x1, blocking collectives: 22.1 us -> 20.5 us  [body(): summed = lax.all_to_all(summed, 'sample', 0, 0)]
  transfers between devices with their start and end apart: 2 -> 2, of which waited for: 1 -> 0; matrix products, arithmetic and copies ran while one was open for 0% -> 0% of each run, Pallas kernels for 2% -> 2%
where the time goes in v3:
time: 76 us; the launch traced here: 75.6 us
  blocking collectives  51 us (67%)
  starting transfers between devices  16.9 us (22%)
  Pallas kernels  6.87 us (9%)
  local copies, waits for them, and re-layouts  0.86 us (1%)
    all_to_all x1, blocking collectives, body(): summed = lax.all_to_all(summed, 'sample', 0, 0)  20.5 us
    all_to_all x1, blocking collectives, body(): lax.all_to_all(partial, 'prefix', 0, 0, axis_index_groups=same_core)  15.9 us
    all_to_all x1, blocking collectives, body(): lax.all_to_all(copies, 'prefix', 0, 0, axis_index_groups=same_core)  14.5 us
    ppermute x1, starting transfers between devices, body(): lax.ppermute(own_queries, ('prefix', 'sample'), [((chip * CORES + core) *...  13.2 us
    ppermute x1, starting transfers between devices, body(): lax.ppermute(held, 'prefix', [(i, i ^ 1) for i in range(CORES * PLANE)])  3.71 us
    pallas_call x1, Pallas kernels, body(): pl.pallas_call(attend_kernel, out_shape=jax.ShapeDtypeStruct((PLANE, BLOC...  3.43 us
    pallas_call x1, Pallas kernels, body(): pl.pallas_call(stage_kernel, out_shape=jax.ShapeDtypeStruct((OWN, SEND_RO...  1.73 us
  transfers between devices with their start and end apart: 2, of which 0 were waited for; matrix products, arithmetic and copies ran while one was open for 0% of the time, Pallas kernels for 2%

profile of v3, /device:TPU:2, one launch (start us, length us, event | category | flops | bytes accessed | tf_op | source)
XLA Modules:
  0.0 75.6 jit_solution(4153973012560226490)
XLA Ops:
  0.0 0.0 copy-start
  0.0 0.8 %copy-done = bf16[4,8192]{1,0:T(4,128)(2,1)S(1)} copy-done((bf16[4,8192]{1,0:T(4,128)(2,1)S(1)}, bf16[4,8192]{1,0:T(4,128)(2,1)}, u32[]{:S(2)}) %copy-start) | copy-done | bytes 65560
  0.9 13.2 %collective-permute-start = (bf16[128,128]{1,0:T(8,128)(2,1)S(1)}, bf16[128,128]{1,0:T(8,128)(2,1)S(1)}, u32[]{:S(2)}, u32[]{:S(2)}) collective-permute-start(bf16[128,128]{1,0:T(8,128)(2,1)S(1)} %query.1), channel_id=1, source_target_pairs={{0,8},{1,9},{2,10},{3,11},{4,12},{5,13},{6,14},{7,15},{8,0},{9,1},... | collective-permute-start | bytes 98312 | tf_op jit(solution)/shard_map/ppermute | solution.py:281
  14.0 1.7 %stage.1.held = bf16[4,336,1024]{2,1,0:T(8,128)(2,1)S(1)} custom-call(s32[4]{0:T(128)} %page_prompt.3, bf16[4,128,1024]{2,1,0:T(8,128)(2,1)} %pool_keys.1, bf16[4,128,1024]{2,1,0:T(8,128)(2,1)} %pool_values.1, bf16[4,32,1024]{2,1,0:T(8,128)(2,1)} %suffix_keys.1, bf16[4,32,1024]{2,1,0:T(8,128)(2,1)} %suffix_values.1), custom_call_target="tpu_custom_call" | custom-call | tf_op jit(solution)/shard_map/stage/pallas_call | solution.py:266
  15.8 0.0 copy-start.1
  15.8 0.0 copy-start.2
  15.8 0.0 copy-start.3
  15.8 3.7 %collective-permute-start.1 = (bf16[4,336,1024]{2,1,0:T(8,128)(2,1)S(1)}, bf16[4,336,1024]{2,1,0:T(8,128)(2,1)S(1)}, u32[]{:S(2)}, u32[]{:S(2)}) collective-permute-start(bf16[4,336,1024]{2,1,0:T(8,128)(2,1)S(1)} %stage.1.held), channel_id=1, source_target_pairs={{0,16},{16,0},{32,48},{48,32},{64,80},{80,64},{96,112},{112,96},{1... | collective-permute-start | bytes 8257544 | tf_op jit(solution)/shard_map/ppermute | solution.py:285
  19.5 0.0 collective-permute-done.shifted
  19.6 0.1 copies.1
  19.7 14.5 %all_to_all.15.queries = bf16[16,128,128]{2,1,0:T(8,128)(2,1)S(1)} all-to-all(bf16[16,128,128]{2,1,0:T(8,128)(2,1)S(1)} %copies.1), channel_id=1, replica_groups={{0,32,64,96,128,160,192,224,256,288,320,352,384,416,448,480},{16,48,80,..., dimensions={0} | all-to-all | bytes 1048576 | tf_op jit(solution)/shard_map/all_to_all | solution.py:296
  34.2 0.0 collective-permute-done.1.got
  34.2 0.0 copy-done.1
  34.2 0.0 copy-done.2
  34.2 0.0 copy-done.3
  34.2 3.4 %attend.1 = bf16[16,144,128]{2,1,0:T(8,128)(2,1)S(1)} custom-call(s32[4]{0:T(128)S(1)} %copy-done.1, s32[4]{0:T(128)S(1)} %copy-done.2, s32[16]{0:T(128)S(1)} %copy-done.3, bf16[16,128,128]{2,1,0:T(8,128)(2,1)S(1)} %all_to_all.15.queries, bf16[4,336,1024]{2,1,0:T(8,128)(2,1)S(1)} %stage.1.held, bf16[4,336,1024]{2,1,0:T(8,128)(2,1)S(1)} %collective-permute-done.1.got), custom_call_target="tpu_custom_call" | custom-call | tf_op jit(solution)/shard_map/attend/pallas_call | solution.py:298
  37.6 15.9 %all_to_all.16.got = bf16[16,144,128]{2,1,0:T(8,128)(2,1)S(1)} all-to-all(bf16[16,144,128]{2,1,0:T(8,128)(2,1)S(1)} %attend.1), channel_id=1, replica_groups={{0,32,64,96,128,160,192,224,256,288,320,352,384,416,448,480},{16,48,80,..., dimensions={0} | all-to-all | bytes 1179648 | tf_op jit(solution)/shard_map/all_to_all | solution.py:310
  53.5 0.8 %plane.1 = bf16[16,16,128]{2,1,0:T(8,128)(2,1)S(1)} custom-call(bf16[16,144,128]{2,1,0:T(8,128)(2,1)S(1)} %all_to_all.16.got), custom_call_target="tpu_custom_call" | custom-call | tf_op jit(solution)/shard_map/plane/pallas_call | solution.py:311
  54.3 20.5 %all_to_all.17.got = bf16[16,16,128]{2,1,0:T(8,128)(2,1)S(1)} all-to-all(bf16[16,16,128]{2,1,0:T(8,128)(2,1)S(1)} %plane.1), channel_id=1, replica_groups=mesh['prefix'=32,'sample'=16] {'sample'}, dimensions={0} | all-to-all | bytes 131072 | tf_op jit(solution)/shard_map/all_to_all | solution.py:319
  74.8 0.8 %final.1 = bf16[4,256]{1,0:T(4,128)(2,1)} custom-call(bf16[16,16,128]{2,1,0:T(8,128)(2,1)S(1)} %all_to_all.17.got), custom_call_target="tpu_custom_call" | custom-call | tf_op jit(solution)/shard_map/final/pallas_call | solution.py:320
  (1 shorter events, 0.0 us)
Async XLA Ops:
  0.0 0.8 %copy-start = (bf16[4,8192]{1,0:T(4,128)(2,1)S(1)}, bf16[4,8192]{1,0:T(4,128)(2,1)}, u32[]{:S(2)}) copy-start(bf16[4,8192]{1,0:T(4,128)(2,1)} %queries.1) | copy-start | bytes 196612
  0.9 18.7 %collective-permute-start = (bf16[128,128]{1,0:T(8,128)(2,1)S(1)}, bf16[128,128]{1,0:T(8,128)(2,1)S(1)}, u32[]{:S(2)}, u32[]{:S(2)}) collective-permute-start(bf16[128,128]{1,0:T(8,128)(2,1)S(1)} %query.1), channel_id=1, source_target_pairs={{0,8},{1,9},{2,10},{3,11},{4,12},{5,13},{6,14},{7,15},{8,0},{9,1},... | collective-permute-start | bytes 98312 | tf_op jit(solution)/shard_map/ppermute | solution.py:281
  15.8 18.4 %copy-start.1 = (s32[4]{0:T(128)S(1)}, s32[4]{0:T(128)}, u32[]{:S(2)}) copy-start(s32[4]{0:T(128)} %page_prompt.3) | copy-start | bytes 52
  15.8 18.4 %copy-start.2 = (s32[4]{0:T(128)S(1)}, s32[4]{0:T(128)}, u32[]{:S(2)}) copy-start(s32[4]{0:T(128)} %suffix_len.1) | copy-start | bytes 52
  15.8 18.4 %copy-start.3 = (s32[16]{0:T(128)S(1)}, s32[16]{0:T(128)}, u32[]{:S(2)}) copy-start(s32[16]{0:T(128)} %constant.2.clone.chip_of) | copy-start | bytes 196
  15.8 18.4 %collective-permute-start.1 = (bf16[4,336,1024]{2,1,0:T(8,128)(2,1)S(1)}, bf16[4,336,1024]{2,1,0:T(8,128)(2,1)S(1)}, u32[]{:S(2)}, u32[]{:S(2)}) collective-permute-start(bf16[4,336,1024]{2,1,0:T(8,128)(2,1)S(1)} %stage.1.held), channel_id=1, source_target_pairs={{0,16},{16,0},{32,48},{48,32},{64,80},{80,64},{96,112},{112,96},{1... | collective-permute-start | bytes 8257544 | tf_op jit(solution)/shard_map/ppermute | solution.py:285

commit v4 on v3

--- a/solution.py
+++ b/solution.py
@@ -1,3 +1,4 @@
+import functools
 import math
 
 import jax
@@ -39,7 +40,10 @@
 BF16 = jnp.bfloat16
 
 
-def query_kernel(queries, out):
+def query_kernel(queries_hbm, out, queries, sem):
+    copy = pltpu.make_async_copy(queries_hbm, queries, sem)
+    copy.start()
+    copy.wait()
     core = lax.rem(lax.axis_index("prefix"), CORES)
     for a in range(KVH):
         parts = []
@@ -90,10 +94,9 @@
     plane = lax.axis_index("sample")
     sign = 1 - 2 * lax.rem(prefix, CORES)
     for a in range(KVH):
-        top[a][...] = jnp.full(top[a].shape, NEG, F32)
-        total[a][...] = jnp.zeros(total[a].shape, F32)
-        acc[a][...] = jnp.zeros(acc[a].shape, F32)
-        peak[a][PROMPTS] = jnp.zeros((HEAD_ROWS, HD), F32)
+        top[a][:PROMPTS] = jnp.full((PROMPTS, HEAD_ROWS, HD), NEG, F32)
+        total[a][:PROMPTS] = jnp.zeros((PROMPTS, HEAD_ROWS, HD), F32)
+        acc[a][:PROMPTS] = jnp.zeros((PROMPTS, HEAD_ROWS, HD), F32)
 
     prompts = [page_prompt[slot] for slot in range(OWN)]
     for slot in range(OWN):
@@ -194,28 +197,30 @@
             out[a * 2 + half, pl.ds(ROWS, STAT_ROWS), :] = packed.astype(BF16)
 
 
+def tree_sum(terms):
+    while len(terms) > 1:
+        terms = [a + b for a, b in zip(terms[::2], terms[1::2])]
+    return terms[0]
+
+
 def plane_kernel(got, out):
     stats = [got[src, pl.ds(ROWS, STAT_ROWS), :].astype(F32) for src in range(PLANE)]
-    best = stats[0]
-    for src in range(1, PLANE):
-        best = jnp.maximum(best, stats[src])
-    denominator = jnp.zeros((STAT_ROWS, HD), F32)
-    sums = [jnp.zeros((8, HD), F32) for _ in range(DEPTH)]
-
+    best = functools.reduce(jnp.maximum, stats)
+    weights = [jnp.exp2(jnp.minimum(stat - best, 0.0)) for stat in stats]
     def column(tile, prompt, quarter):
         rows, start = quarter // 2 * 8, quarter % 2 * 16 + prompt
         return tile[rows:rows + 8, start:start + 1]
 
-    for src in range(PLANE):
-        weight = jnp.exp2(jnp.minimum(stats[src] - best, 0.0))
-        part = pltpu.roll(stats[src], HD - 4, 1) + pltpu.roll(stats[src], HD - 8, 1)
-        denominator = denominator + weight * part
-        for prompt in range(PROMPTS):
-            tile = got[src, pl.ds(prompt * 32, 32), :].astype(F32)
-            for quarter in range(4):
-                i = prompt * 4 + quarter
-                sums[i] = sums[i] + (
-                    tile[quarter * 8:quarter * 8 + 8] * column(weight, prompt, quarter))
+    denominator = tree_sum([
+        weight * (pltpu.roll(stat, HD - 4, 1) + pltpu.roll(stat, HD - 8, 1))
+        for weight, stat in zip(weights, stats)])
+    sums = []
+    for prompt in range(PROMPTS):
+        tiles = [got[src, pl.ds(prompt * 32, 32), :].astype(F32) for src in range(PLANE)]
+        for quarter in range(4):
+            rows = slice(quarter * 8, quarter * 8 + 8)
+            sums.append(tree_sum([tile[rows] * column(weight, prompt, quarter)
+                                  for tile, weight in zip(tiles, weights)]))
     high = denominator.astype(BF16).astype(F32)
     lane = lax.broadcasted_iota(jnp.int32, (8, HD), 1)
     for prompt in range(PROMPTS):
@@ -258,11 +263,12 @@
     own_queries = pl.pallas_call(
         query_kernel,
         out_shape=jax.ShapeDtypeStruct((ROWS, HD), BF16),
-        in_specs=[VMEM],
-        out_specs=VMEM,
+        in_specs=[ANY],
+        out_specs=VMEM,
+        scratch_shapes=[pltpu.VMEM((OWN, H * HD), BF16), pltpu.SemaphoreType.DMA],
         compiler_params=budget(2),
         name="query",
-    )(queries)
+    )(pltpu.with_memory_space_constraint(queries, pltpu.HBM))
     held = pl.pallas_call(
         stage_kernel,
         out_shape=jax.ShapeDtypeStruct((OWN, SEND_ROWS, KVH * HD), BF16),

time: 76 us -> 75.6 us (level)
  local copies, waits for them, and re-layouts: 0.86 us -> 0.02 us
    pallas_call x1, Pallas kernels: 0.04 us -> 0.88 us  [body(): pl.pallas_call(query_kernel, out_shape=jax.ShapeDtypeStruct((ROWS, HD), B...]
    unnamed x8 -> x6, local copies, waits for them, and re-layouts: 0.86 us -> 0.02 us
where the time goes in v4:
time: 75.6 us; the launch traced here: 75.2 us
  blocking collectives  51 us (67%)
  starting transfers between devices  16.9 us (22%)
  Pallas kernels  7.3 us (10%)
    all_to_all x1, blocking collectives, body(): summed = lax.all_to_all(summed, 'sample', 0, 0)  20.5 us
    all_to_all x1, blocking collectives, body(): lax.all_to_all(partial, 'prefix', 0, 0, axis_index_groups=same_core)  15.9 us
    all_to_all x1, blocking collectives, body(): lax.all_to_all(copies, 'prefix', 0, 0, axis_index_groups=same_core)  14.5 us
    ppermute x1, starting transfers between devices, body(): lax.ppermute(own_queries, ('prefix', 'sample'), [((chip * CORES + core) *...  13.2 us
    ppermute x1, starting transfers between devices, body(): lax.ppermute(held, 'prefix', [(i, i ^ 1) for i in range(CORES * PLANE)])  3.71 us
    pallas_call x1, Pallas kernels, body(): pl.pallas_call(attend_kernel, out_shape=jax.ShapeDtypeStruct((PLANE, BLOC...  3.34 us
    pallas_call x1, Pallas kernels, body(): pl.pallas_call(stage_kernel, out_shape=jax.ShapeDtypeStruct((OWN, SEND_RO...  1.73 us
  transfers between devices with their start and end apart: 2, of which 0 were waited for; matrix products, arithmetic and copies ran while one was open for 0% of the time, Pallas kernels for 2%

profile of v4, /device:TPU:2, one launch (start us, length us, event | category | flops | bytes accessed | tf_op | source)
XLA Modules:
  0.0 75.2 jit_solution(10716610245877322937)
XLA Ops:
  0.0 0.9 %query.1 = bf16[128,128]{1,0:T(8,128)(2,1)S(1)} custom-call(bf16[4,8192]{1,0:T(4,128)(2,1)} %queries_hbm.1), custom_call_target="tpu_custom_call" | custom-call | tf_op jit(solution)/shard_map/query/pallas_call | solution.py:263
  0.9 13.2 %collective-permute-start = (bf16[128,128]{1,0:T(8,128)(2,1)S(1)}, bf16[128,128]{1,0:T(8,128)(2,1)S(1)}, u32[]{:S(2)}, u32[]{:S(2)}) collective-permute-start(bf16[128,128]{1,0:T(8,128)(2,1)S(1)} %query.1), channel_id=1, source_target_pairs={{0,8},{1,9},{2,10},{3,11},{4,12},{5,13},{6,14},{7,15},{8,0},{9,1},... | collective-permute-start | bytes 98312 | tf_op jit(solution)/shard_map/ppermute | solution.py:287
  14.1 1.7 %stage.1.held = bf16[4,336,1024]{2,1,0:T(8,128)(2,1)S(1)} custom-call(s32[4]{0:T(128)} %page_prompt.3, bf16[4,128,1024]{2,1,0:T(8,128)(2,1)} %pool_keys.1, bf16[4,128,1024]{2,1,0:T(8,128)(2,1)} %pool_values.1, bf16[4,32,1024]{2,1,0:T(8,128)(2,1)} %suffix_keys.1, bf16[4,32,1024]{2,1,0:T(8,128)(2,1)} %suffix_values.1), custom_call_target="tpu_custom_call" | custom-call | tf_op jit(solution)/shard_map/stage/pallas_call | solution.py:272
  15.8 0.0 copy-start
  15.8 0.0 copy-start.1
  15.8 0.0 copy-start.2
  15.8 3.7 %collective-permute-start.1 = (bf16[4,336,1024]{2,1,0:T(8,128)(2,1)S(1)}, bf16[4,336,1024]{2,1,0:T(8,128)(2,1)S(1)}, u32[]{:S(2)}, u32[]{:S(2)}) collective-permute-start(bf16[4,336,1024]{2,1,0:T(8,128)(2,1)S(1)} %stage.1.held), channel_id=1, source_target_pairs={{0,16},{16,0},{32,48},{48,32},{64,80},{80,64},{96,112},{112,96},{1... | collective-permute-start | bytes 8257544 | tf_op jit(solution)/shard_map/ppermute | solution.py:291
  19.6 0.0 collective-permute-done.shifted
  19.6 0.1 copies.1
  19.7 14.5 %all_to_all.15.queries = bf16[16,128,128]{2,1,0:T(8,128)(2,1)S(1)} all-to-all(bf16[16,128,128]{2,1,0:T(8,128)(2,1)S(1)} %copies.1), channel_id=1, replica_groups={{0,32,64,96,128,160,192,224,256,288,320,352,384,416,448,480},{16,48,80,..., dimensions={0} | all-to-all | bytes 1048576 | tf_op jit(solution)/shard_map/all_to_all | solution.py:302
  34.2 0.0 collective-permute-done.1.got
  34.2 0.0 copy-done
  34.2 0.0 copy-done.1
  34.2 0.0 copy-done.2
  34.2 3.3 %attend.1 = bf16[16,144,128]{2,1,0:T(8,128)(2,1)S(1)} custom-call(s32[4]{0:T(128)S(1)} %copy-done, s32[4]{0:T(128)S(1)} %copy-done.1, s32[16]{0:T(128)S(1)} %copy-done.2, bf16[16,128,128]{2,1,0:T(8,128)(2,1)S(1)} %all_to_all.15.queries, bf16[4,336,1024]{2,1,0:T(8,128)(2,1)S(1)} %stage.1.held, bf16[4,336,1024]{2,1,0:T(8,128)(2,1)S(1)} %collective-permute-done.1.got), custom_call_target="tpu_custom_call" | custom-call | tf_op jit(solution)/shard_map/attend/pallas_call | solution.py:304
  37.6 15.9 %all_to_all.16.got = bf16[16,144,128]{2,1,0:T(8,128)(2,1)S(1)} all-to-all(bf16[16,144,128]{2,1,0:T(8,128)(2,1)S(1)} %attend.1), channel_id=1, replica_groups={{0,32,64,96,128,160,192,224,256,288,320,352,384,416,448,480},{16,48,80,..., dimensions={0} | all-to-all | bytes 1179648 | tf_op jit(solution)/shard_map/all_to_all | solution.py:316
  53.5 0.4 plane.1
  53.9 20.5 %all_to_all.17.got = bf16[16,16,128]{2,1,0:T(8,128)(2,1)S(1)} all-to-all(bf16[16,16,128]{2,1,0:T(8,128)(2,1)S(1)} %plane.1), channel_id=1, replica_groups=mesh['prefix'=32,'sample'=16] {'sample'}, dimensions={0} | all-to-all | bytes 131072 | tf_op jit(solution)/shard_map/all_to_all | solution.py:325
  74.4 0.8 %final.1 = bf16[4,256]{1,0:T(4,128)(2,1)} custom-call(bf16[16,16,128]{2,1,0:T(8,128)(2,1)S(1)} %all_to_all.17.got), custom_call_target="tpu_custom_call" | custom-call | tf_op jit(solution)/shard_map/final/pallas_call | solution.py:326
Async XLA Ops:
  0.9 18.7 %collective-permute-start = (bf16[128,128]{1,0:T(8,128)(2,1)S(1)}, bf16[128,128]{1,0:T(8,128)(2,1)S(1)}, u32[]{:S(2)}, u32[]{:S(2)}) collective-permute-start(bf16[128,128]{1,0:T(8,128)(2,1)S(1)} %query.1), channel_id=1, source_target_pairs={{0,8},{1,9},{2,10},{3,11},{4,12},{5,13},{6,14},{7,15},{8,0},{9,1},... | collective-permute-start | bytes 98312 | tf_op jit(solution)/shard_map/ppermute | solution.py:287
  15.8 18.4 %copy-start = (s32[4]{0:T(128)S(1)}, s32[4]{0:T(128)}, u32[]{:S(2)}) copy-start(s32[4]{0:T(128)} %page_prompt.3) | copy-start | bytes 52
  15.8 18.4 %copy-start.1 = (s32[4]{0:T(128)S(1)}, s32[4]{0:T(128)}, u32[]{:S(2)}) copy-start(s32[4]{0:T(128)} %suffix_len.1) | copy-start | bytes 52
  15.8 18.4 %copy-start.2 = (s32[16]{0:T(128)S(1)}, s32[16]{0:T(128)}, u32[]{:S(2)}) copy-start(s32[16]{0:T(128)} %constant.2.clone.chip_of) | copy-start | bytes 196
  15.8 18.4 %collective-permute-start.1 = (bf16[4,336,1024]{2,1,0:T(8,128)(2,1)S(1)}, bf16[4,336,1024]{2,1,0:T(8,128)(2,1)S(1)}, u32[]{:S(2)}, u32[]{:S(2)}) collective-permute-start(bf16[4,336,1024]{2,1,0:T(8,128)(2,1)S(1)} %stage.1.held), channel_id=1, source_target_pairs={{0,16},{16,0},{32,48},{48,32},{64,80},{80,64},{96,112},{112,96},{1... | collective-permute-start | bytes 8257544 | tf_op jit(solution)/shard_map/ppermute | solution.py:291

commit v5 on v4

--- a/solution.py
+++ b/solution.py
@@ -35,7 +35,10 @@
 CHIP_ORDER = (0, 4, 1, 2, 8, 3, 12, 5, 6, 9, 13, 7, 14, 11, 10, 15)
 DISTANCES = (8, 7, 9, 6, 10, 5, 11, 4, 12, 3, 13, 2, 14, 1, 15, 0)
 DISTANCE_OF = dict(zip(CHIP_ORDER, DISTANCES))
-CHIP_OF = dict(zip(DISTANCES, CHIP_ORDER))
+CHIP_GROUP = tuple(range(10, PLANE)) + tuple(range(10))
+PLANE_GROUP = tuple(range(8, DEPTH)) + tuple(range(8))
+QUERY_GROUP = tuple(range(0, PLANE)) + tuple(range(0))
+CHIP_OF = {distance: QUERY_GROUP.index(chip) for distance, chip in zip(DISTANCES, CHIP_ORDER)}
 F32 = jnp.float32
 BF16 = jnp.bfloat16
 
@@ -187,14 +190,15 @@
         for half in range(2):
             def quarter_rows(tile, q):
                 return tile[q * 16 + half * 8:q * 16 + half * 8 + 8]
+            owner = CHIP_GROUP.index(a * 2 + half)
             for prompt in range(PROMPTS):
                 sums = acc[a][prompt]
                 rows = jnp.concatenate([quarter_rows(sums, q) for q in range(4)], axis=0)
-                out[a * 2 + half, pl.ds(prompt * 32, 32), :] = rows.astype(BF16)
+                out[owner, pl.ds(prompt * 32, 32), :] = rows.astype(BF16)
             packed = jnp.concatenate(
                 [quarter_rows(stats, q) + pltpu.roll(quarter_rows(stats, q + 1), 16, 1)
                  for q in (0, 2)], axis=0)
-            out[a * 2 + half, pl.ds(ROWS, STAT_ROWS), :] = packed.astype(BF16)
+            out[owner, pl.ds(ROWS, STAT_ROWS), :] = packed.astype(BF16)
 
 
 def tree_sum(terms):
@@ -230,7 +234,7 @@
                 lane == 0, column(best, prompt, quarter),
                 jnp.where(lane == 1, column(high, prompt, quarter),
                           column(denominator - high, prompt, quarter)))
-            out[i] = jnp.concatenate([sums[i], stat], axis=0).astype(BF16)
+            out[PLANE_GROUP.index(i)] = jnp.concatenate([sums[i], stat], axis=0).astype(BF16)
 
 
 def final_kernel(got, out):
@@ -289,7 +293,7 @@
         [((chip * CORES + core) * DEPTH + z, (chip * CORES + core) * DEPTH + (z + (1 - 2 * core) * DISTANCE_OF[chip]) % DEPTH)
          for chip in range(PLANE) for core in range(CORES) for z in range(DEPTH)])
     got = lax.ppermute(held, "prefix", [(i, i ^ 1) for i in range(CORES * PLANE)])
-    same_core = [[chip * CORES + core for chip in range(PLANE)] for core in range(CORES)]
+    same_core = [[chip * CORES + core for chip in CHIP_GROUP] for core in range(CORES)]
     copies = pl.pallas_call(
         copy_kernel,
         out_shape=jax.ShapeDtypeStruct((PLANE, ROWS, HD), BF16),
@@ -299,7 +303,9 @@
         cost_estimate=pl.CostEstimate(flops=10**11, transcendentals=0, bytes_accessed=MIB),
         name="copies",
     )(shifted)
-    every_query = lax.all_to_all(copies, "prefix", 0, 0, axis_index_groups=same_core)
+    every_query = lax.all_to_all(
+        copies, "prefix", 0, 0,
+        axis_index_groups=[[chip * CORES + core for chip in QUERY_GROUP] for core in range(CORES)])
     chip_of = jnp.array([CHIP_OF[distance] for distance in range(DEPTH)], jnp.int32)
     partial = pl.pallas_call(
         attend_kernel,
@@ -322,7 +328,7 @@
         compiler_params=budget(4),
         name="plane",
     )(partial)
-    summed = lax.all_to_all(summed, "sample", 0, 0)
+    summed = lax.all_to_all(summed, "sample", 0, 0, axis_index_groups=[list(PLANE_GROUP)])
     return pl.pallas_call(
         final_kernel,
         out_shape=jax.ShapeDtypeStruct((OWN, 2 * HD), BF16),

time: 75.6 us -> 69.1 us (0.914)
  blocking collectives: 51 us -> 44.5 us
    all_to_all x2, blocking collectives: 35.1 us -> 30.1 us  [the longest x1 15.5 us: body(): lax.all_to_all(summed, 'sample', 0, 0, axis_index_groups=[list(PLANE_GROU...]
    all_to_all x1, blocking collectives: 15.9 us -> 14.4 us  [body(): lax.all_to_all(partial, 'prefix', 0, 0, axis_index_groups=same_core)]
  transfers between devices with their start and end apart: 2 -> 2, of which waited for: 0 -> 0; matrix products, arithmetic and copies ran while one was open for 0% -> 0% of each run, Pallas kernels for 2% -> 3%
where the time goes in v5:
time: 69.1 us; the launch traced here: 68.8 us
  blocking collectives  44.5 us (64%)
  starting transfers between devices  16.9 us (24%)
  Pallas kernels  7.3 us (11%)
    all_to_all x1, blocking collectives, body(): lax.all_to_all(summed, 'sample', 0, 0, axis_index_groups=[list(PLANE_GROU...  15.5 us
    all_to_all x1, blocking collectives, body(): lax.all_to_all(copies, 'prefix', 0, 0, axis_index_groups=[[chip * CORES +...  14.5 us
    all_to_all x1, blocking collectives, body(): lax.all_to_all(partial, 'prefix', 0, 0, axis_index_groups=same_core)  14.4 us
    ppermute x1, starting transfers between devices, body(): lax.ppermute(own_queries, ('prefix', 'sample'), [((chip * CORES + core) *...  13.2 us
    ppermute x1, starting transfers between devices, body(): lax.ppermute(held, 'prefix', [(i, i ^ 1) for i in range(CORES * PLANE)])  3.71 us
    pallas_call x1, Pallas kernels, body(): pl.pallas_call(attend_kernel, out_shape=jax.ShapeDtypeStruct((PLANE, BLOC...  3.34 us
    pallas_call x1, Pallas kernels, body(): pl.pallas_call(stage_kernel, out_shape=jax.ShapeDtypeStruct((OWN, SEND_RO...  1.73 us
  transfers between devices with their start and end apart: 2, of which 0 were waited for; matrix products, arithmetic and copies ran while one was open for 0% of the time, Pallas kernels for 3%

profile of v5, /device:TPU:2, one launch (start us, length us, event | category | flops | bytes accessed | tf_op | source)
XLA Modules:
  0.0 68.8 jit_solution(9874738781764195407)
XLA Ops:
  0.0 0.9 %query.1 = bf16[128,128]{1,0:T(8,128)(2,1)S(1)} custom-call(bf16[4,8192]{1,0:T(4,128)(2,1)} %queries_hbm.1), custom_call_target="tpu_custom_call" | custom-call | tf_op jit(solution)/shard_map/query/pallas_call | solution.py:267
  0.9 13.2 %collective-permute-start = (bf16[128,128]{1,0:T(8,128)(2,1)S(1)}, bf16[128,128]{1,0:T(8,128)(2,1)S(1)}, u32[]{:S(2)}, u32[]{:S(2)}) collective-permute-start(bf16[128,128]{1,0:T(8,128)(2,1)S(1)} %query.1), channel_id=1, source_target_pairs={{0,8},{1,9},{2,10},{3,11},{4,12},{5,13},{6,14},{7,15},{8,0},{9,1},... | collective-permute-start | bytes 98312 | tf_op jit(solution)/shard_map/ppermute | solution.py:291
  14.1 1.7 %stage.1.held = bf16[4,336,1024]{2,1,0:T(8,128)(2,1)S(1)} custom-call(s32[4]{0:T(128)} %page_prompt.3, bf16[4,128,1024]{2,1,0:T(8,128)(2,1)} %pool_keys.1, bf16[4,128,1024]{2,1,0:T(8,128)(2,1)} %pool_values.1, bf16[4,32,1024]{2,1,0:T(8,128)(2,1)} %suffix_keys.1, bf16[4,32,1024]{2,1,0:T(8,128)(2,1)} %suffix_values.1), custom_call_target="tpu_custom_call" | custom-call | tf_op jit(solution)/shard_map/stage/pallas_call | solution.py:276
  15.8 0.0 copy-start
  15.8 0.0 copy-start.1
  15.8 0.0 copy-start.2
  15.8 3.7 %collective-permute-start.1 = (bf16[4,336,1024]{2,1,0:T(8,128)(2,1)S(1)}, bf16[4,336,1024]{2,1,0:T(8,128)(2,1)S(1)}, u32[]{:S(2)}, u32[]{:S(2)}) collective-permute-start(bf16[4,336,1024]{2,1,0:T(8,128)(2,1)S(1)} %stage.1.held), channel_id=1, source_target_pairs={{0,16},{16,0},{32,48},{48,32},{64,80},{80,64},{96,112},{112,96},{1... | collective-permute-start | bytes 8257544 | tf_op jit(solution)/shard_map/ppermute | solution.py:295
  19.6 0.0 collective-permute-done.shifted
  19.6 0.1 copies.1
  19.7 14.5 %all_to_all.15.queries = bf16[16,128,128]{2,1,0:T(8,128)(2,1)S(1)} all-to-all(bf16[16,128,128]{2,1,0:T(8,128)(2,1)S(1)} %copies.1), channel_id=1, replica_groups={{0,32,64,96,128,160,192,224,256,288,320,352,384,416,448,480},{16,48,80,..., dimensions={0} | all-to-all | bytes 1048576 | tf_op jit(solution)/shard_map/all_to_all | solution.py:306
  34.2 0.0 collective-permute-done.1.got
  34.2 0.0 copy-done
  34.2 0.0 copy-done.1
  34.2 0.0 copy-done.2
  34.2 3.3 %attend.1 = bf16[16,144,128]{2,1,0:T(8,128)(2,1)S(1)} custom-call(s32[4]{0:T(128)S(1)} %copy-done, s32[4]{0:T(128)S(1)} %copy-done.1, s32[16]{0:T(128)S(1)} %copy-done.2, bf16[16,128,128]{2,1,0:T(8,128)(2,1)S(1)} %all_to_all.15.queries, bf16[4,336,1024]{2,1,0:T(8,128)(2,1)S(1)} %stage.1.held, bf16[4,336,1024]{2,1,0:T(8,128)(2,1)S(1)} %collective-permute-done.1.got), custom_call_target="tpu_custom_call" | custom-call | tf_op jit(solution)/shard_map/attend/pallas_call | solution.py:310
  37.6 14.4 %all_to_all.16.got = bf16[16,144,128]{2,1,0:T(8,128)(2,1)S(1)} all-to-all(bf16[16,144,128]{2,1,0:T(8,128)(2,1)S(1)} %attend.1), channel_id=1, replica_groups={{320,352,384,416,448,480,0,32,64,96,128,160,192,224,256,288},{336,368,4..., dimensions={0} | all-to-all | bytes 1179648 | tf_op jit(solution)/shard_map/all_to_all | solution.py:322
  52.0 0.4 plane.1
  52.4 15.5 %all_to_all.17.got = bf16[16,16,128]{2,1,0:T(8,128)(2,1)S(1)} all-to-all(bf16[16,16,128]{2,1,0:T(8,128)(2,1)S(1)} %plane.1), channel_id=1, replica_groups={{8,9,10,11,12,13,14,15,0,1,2,3,4,5,6,7},{24,25,26,27,28,29,30,31,16,17,..., dimensions={0} | all-to-all | bytes 131072 | tf_op jit(solution)/shard_map/all_to_all | solution.py:331
  67.9 0.8 %final.1 = bf16[4,256]{1,0:T(4,128)(2,1)} custom-call(bf16[16,16,128]{2,1,0:T(8,128)(2,1)S(1)} %all_to_all.17.got), custom_call_target="tpu_custom_call" | custom-call | tf_op jit(solution)/shard_map/final/pallas_call | solution.py:332
Async XLA Ops:
  0.9 18.7 %collective-permute-start = (bf16[128,128]{1,0:T(8,128)(2,1)S(1)}, bf16[128,128]{1,0:T(8,128)(2,1)S(1)}, u32[]{:S(2)}, u32[]{:S(2)}) collective-permute-start(bf16[128,128]{1,0:T(8,128)(2,1)S(1)} %query.1), channel_id=1, source_target_pairs={{0,8},{1,9},{2,10},{3,11},{4,12},{5,13},{6,14},{7,15},{8,0},{9,1},... | collective-permute-start | bytes 98312 | tf_op jit(solution)/shard_map/ppermute | solution.py:291
  15.8 18.4 %copy-start = (s32[4]{0:T(128)S(1)}, s32[4]{0:T(128)}, u32[]{:S(2)}) copy-start(s32[4]{0:T(128)} %page_prompt.3) | copy-start | bytes 52
  15.8 18.4 %copy-start.1 = (s32[4]{0:T(128)S(1)}, s32[4]{0:T(128)}, u32[]{:S(2)}) copy-start(s32[4]{0:T(128)} %suffix_len.1) | copy-start | bytes 52
  15.8 18.4 %copy-start.2 = (s32[16]{0:T(128)S(1)}, s32[16]{0:T(128)}, u32[]{:S(2)}) copy-start(s32[16]{0:T(128)} %constant.2.clone.chip_of) | copy-start | bytes 196
  15.8 18.4 %collective-permute-start.1 = (bf16[4,336,1024]{2,1,0:T(8,128)(2,1)S(1)}, bf16[4,336,1024]{2,1,0:T(8,128)(2,1)S(1)}, u32[]{:S(2)}, u32[]{:S(2)}) collective-permute-start(bf16[4,336,1024]{2,1,0:T(8,128)(2,1)S(1)} %stage.1.held), channel_id=1, source_target_pairs={{0,16},{16,0},{32,48},{48,32},{64,80},{80,64},{96,112},{112,96},{1... | collective-permute-start | bytes 8257544 | tf_op jit(solution)/shard_map/ppermute | solution.py:295

commit v6 on v5

--- a/solution.py
+++ b/solution.py
@@ -37,35 +37,15 @@
 DISTANCE_OF = dict(zip(CHIP_ORDER, DISTANCES))
 CHIP_GROUP = tuple(range(10, PLANE)) + tuple(range(10))
 PLANE_GROUP = tuple(range(8, DEPTH)) + tuple(range(8))
-QUERY_GROUP = tuple(range(0, PLANE)) + tuple(range(0))
+QUERY_GROUP = tuple(range(1, PLANE)) + tuple(range(1))
 CHIP_OF = {distance: QUERY_GROUP.index(chip) for distance, chip in zip(DISTANCES, CHIP_ORDER)}
+EARLY_PLANES = 7
 F32 = jnp.float32
 BF16 = jnp.bfloat16
 
 
-def query_kernel(queries_hbm, out, queries, sem):
-    copy = pltpu.make_async_copy(queries_hbm, queries, sem)
-    copy.start()
-    copy.wait()
-    core = lax.rem(lax.axis_index("prefix"), CORES)
-    for a in range(KVH):
-        parts = []
-        for half in range(2):
-            for mate in range(2):
-                head = a * 8 + half * 4 + mate
-                column = pl.multiple_of(head * HD + core * (2 * HD), HD)
-                parts.append(queries[:, pl.ds(column, HD)].astype(F32))
-        out[pl.ds(a * 16, 16), :] = jnp.concatenate(parts, axis=0).astype(BF16)
-
-
-def copy_kernel(shifted, out):
-    rows = shifted[...]
-    for chip in range(PLANE):
-        out[chip] = rows
-
-
-def stage_kernel(page_prompt, pool_keys, pool_values, suffix_keys, suffix_values, out,
-                 keys, suffix, prompts, sems):
+def stage(page_prompt, pool_keys, pool_values, suffix_keys, suffix_values, out,
+          keys, suffix, prompts, sems):
     pieces = ((page_prompt, prompts), (pool_keys, keys), (suffix_keys, suffix),
               (pool_values, out.at[:, pl.ds(VALUE_ROW, PAGE), :]),
               (suffix_values, out.at[:, pl.ds(SUFFIX_VALUE_ROW, SPAN), :]))
@@ -88,6 +68,39 @@
         out[:, pl.ds(SUFFIX_KEY_ROW, SPAN), head] = turned.reshape(OWN, SPAN, OWN * SPAN)
     for copy in copies[3:]:
         copy.wait()
+
+
+def query_kernel(queries_hbm, page_prompt, pool_keys, pool_values, suffix_keys, suffix_values,
+                 out, held, queries, sem, *scratch):
+    copy = pltpu.make_async_copy(queries_hbm, queries, sem)
+    copy.start()
+    copy.wait()
+    core = lax.rem(lax.axis_index("prefix"), CORES)
+    for a in range(KVH):
+        parts = []
+        for half in range(2):
+            for mate in range(2):
+                head = a * 8 + half * 4 + mate
+                column = pl.multiple_of(head * HD + core * (2 * HD), HD)
+                parts.append(queries[:, pl.ds(column, HD)].astype(F32))
+        out[pl.ds(a * 16, 16), :] = jnp.concatenate(parts, axis=0).astype(BF16)
+
+    @pl.when(lax.axis_index("sample") < EARLY_PLANES)
+    def _():
+        stage(page_prompt, pool_keys, pool_values, suffix_keys, suffix_values, held, *scratch)
+
+
+def stage_kernel(page_prompt, pool_keys, pool_values, suffix_keys, suffix_values, held, out,
+                 *scratch):
+    @pl.when(lax.axis_index("sample") >= EARLY_PLANES)
+    def _():
+        stage(page_prompt, pool_keys, pool_values, suffix_keys, suffix_values, out, *scratch)
+
+
+def copy_kernel(shifted, out):
+    rows = shifted[...]
+    for chip in range(PLANE):
+        out[chip] = rows
 
 
 def attend_kernel(page_prompt, suffix_len, chip_of, queries, held, got, out, scores,
@@ -264,30 +277,37 @@
 
 
 def body(queries, pool_keys, pool_values, page_prompt, suffix_keys, suffix_values, suffix_len):
-    own_queries = pl.pallas_call(
+    def pages():
+        return tuple(
+            pltpu.with_memory_space_constraint(array, pltpu.HBM)
+            for array in (page_prompt, pool_keys, pool_values, suffix_keys, suffix_values))
+
+    room = [
+        pltpu.VMEM((OWN, PAGE, KVH * HD), BF16),
+        pltpu.VMEM((OWN, SPAN, KVH * HD), BF16),
+        pltpu.SMEM((OWN,), jnp.int32),
+        pltpu.SemaphoreType.DMA((5,)),
+    ]
+    held_shape = jax.ShapeDtypeStruct((OWN, SEND_ROWS, KVH * HD), BF16)
+    own_queries, held = pl.pallas_call(
         query_kernel,
-        out_shape=jax.ShapeDtypeStruct((ROWS, HD), BF16),
-        in_specs=[ANY],
-        out_specs=VMEM,
-        scratch_shapes=[pltpu.VMEM((OWN, H * HD), BF16), pltpu.SemaphoreType.DMA],
-        compiler_params=budget(2),
+        out_shape=(jax.ShapeDtypeStruct((ROWS, HD), BF16), held_shape),
+        in_specs=[ANY] * 6,
+        out_specs=(VMEM, VMEM),
+        scratch_shapes=[pltpu.VMEM((OWN, H * HD), BF16), pltpu.SemaphoreType.DMA] + room,
+        compiler_params=budget(6),
         name="query",
-    )(pltpu.with_memory_space_constraint(queries, pltpu.HBM))
+    )(pltpu.with_memory_space_constraint(queries, pltpu.HBM), *pages())
     held = pl.pallas_call(
         stage_kernel,
-        out_shape=jax.ShapeDtypeStruct((OWN, SEND_ROWS, KVH * HD), BF16),
-        in_specs=[ANY] * 5,
-        out_specs=VMEM,
-        scratch_shapes=[
-            pltpu.VMEM((OWN, PAGE, KVH * HD), BF16),
-            pltpu.VMEM((OWN, SPAN, KVH * HD), BF16),
-            pltpu.SMEM((OWN,), jnp.int32),
-            pltpu.SemaphoreType.DMA((5,)),
-        ],
+        out_shape=held_shape,
+        in_specs=[ANY] * 5 + [VMEM],
+        out_specs=VMEM,
+        input_output_aliases={5: 0},
+        scratch_shapes=room,
         compiler_params=budget(6),
         name="stage",
-    )(*(pltpu.with_memory_space_constraint(array, pltpu.HBM)
-        for array in (page_prompt, pool_keys, pool_values, suffix_keys, suffix_values)))
+    )(*pages(), held)
     shifted = lax.ppermute(
         own_queries, ("prefix", "sample"),
         [((chip * CORES + core) * DEPTH + z, (chip * CORES + core) * DEPTH + (z + (1 - 2 * core) * DISTANCE_OF[chip]) % DEPTH)

time: 69.1 us -> 68.1 us (0.986)
  starting transfers between devices: 16.9 us -> 15.2 us
    ppermute x1, starting transfers between devices: 13.2 us -> 11.5 us  [body(): lax.ppermute(own_queries, ('prefix', 'sample'), [((chip * CORES + core) *...]
  transfers between devices with their start and end apart: 2 -> 2, of which waited for: 0 -> 1; matrix products, arithmetic and copies ran while one was open for 0% -> 0% of each run, Pallas kernels for 3% -> 0%
where the time goes in v6:
time: 68.1 us; the launch traced here: 67.8 us
  blocking collectives  44.9 us (66%)
  starting transfers between devices  15.2 us (22%)
  Pallas kernels  7.35 us (11%)
    all_to_all x1, blocking collectives, body(): lax.all_to_all(summed, 'sample', 0, 0, axis_index_groups=[list(PLANE_GROU...  16 us
    all_to_all x1, blocking collectives, body(): lax.all_to_all(copies, 'prefix', 0, 0, axis_index_groups=[[chip * CORES +...  15.2 us
    all_to_all x1, blocking collectives, body(): lax.all_to_all(partial, 'prefix', 0, 0, axis_index_groups=same_core)  13.7 us
    ppermute x1, starting transfers between devices, body(): lax.ppermute(own_queries, ('prefix', 'sample'), [((chip * CORES + core) *...  11.5 us
    ppermute x1, starting transfers between devices, body(): lax.ppermute(held, 'prefix', [(i, i ^ 1) for i in range(CORES * PLANE)])  3.71 us
    pallas_call x1, Pallas kernels, body(): pl.pallas_call(attend_kernel, out_shape=jax.ShapeDtypeStruct((PLANE, BLOC...  3.34 us
    pallas_call x1, Pallas kernels, body(): pl.pallas_call(query_kernel, out_shape=(jax.ShapeDtypeStruct((ROWS, HD),...  2.6 us
  transfers between devices with their start and end apart: 2, of which 1 were waited for; matrix products, arithmetic and copies ran while one was open for 0% of the time, Pallas kernels for 0%

profile of v6, /device:TPU:2, one launch (start us, length us, event | category | flops | bytes accessed | tf_op | source)
XLA Modules:
  0.0 67.8 jit_solution(9622712200794480943)
XLA Ops:
  0.0 2.6 %query.1 = (bf16[128,128]{1,0:T(8,128)(2,1)S(1)}, bf16[4,336,1024]{2,1,0:T(8,128)(2,1)S(1)}) custom-call(bf16[4,8192]{1,0:T(4,128)(2,1)} %queries_hbm.1, s32[4]{0:T(128)} %page_prompt.5, bf16[4,128,1024]{2,1,0:T(8,128)(2,1)} %pool_keys.3, bf16[4,128,1024]{2,1,0:T(8,128)(2,1)} %pool_values.3, bf16[4,32,1024]{2,1,0:T(8,128)(2,1)} %suffix_keys.3, ...), custom_call_target="tpu_custom_call" | custom-call | tf_op jit(solution)/shard_map/query/pallas_call | solution.py:292
  2.6 11.5 %collective-permute-start = (bf16[128,128]{1,0:T(8,128)(2,1)S(1)}, bf16[128,128]{1,0:T(8,128)(2,1)S(1)}, u32[]{:S(2)}, u32[]{:S(2)}) collective-permute-start(bf16[128,128]{1,0:T(8,128)(2,1)S(1)} %get-tuple-element.7), channel_id=1, source_target_pairs={{0,8},{1,9},{2,10},{3,11},{4,12},{5,13},{6,14},{7,15},{8,0},{9,1},... | collective-permute-start | bytes 98312 | tf_op jit(solution)/shard_map/ppermute | solution.py:311
  14.1 0.1 stage.1.held
  14.2 0.0 copy-start
  14.2 0.0 copy-start.1
  14.2 0.0 copy-start.2
  14.2 3.7 %collective-permute-start.1 = (bf16[4,336,1024]{2,1,0:T(8,128)(2,1)S(1)}, bf16[4,336,1024]{2,1,0:T(8,128)(2,1)S(1)}, u32[]{:S(2)}, u32[]{:S(2)}) collective-permute-start(bf16[4,336,1024]{2,1,0:T(8,128)(2,1)S(1)} %stage.1.held), channel_id=1, source_target_pairs={{0,16},{16,0},{32,48},{48,32},{64,80},{80,64},{96,112},{112,96},{1... | collective-permute-start | bytes 8257544 | tf_op jit(solution)/shard_map/ppermute | solution.py:315
  17.9 0.3 collective-permute-done.shifted
  18.2 0.1 copies.1
  18.3 15.2 %all_to_all.15.queries = bf16[16,128,128]{2,1,0:T(8,128)(2,1)S(1)} all-to-all(bf16[16,128,128]{2,1,0:T(8,128)(2,1)S(1)} %copies.1), channel_id=1, replica_groups={{32,64,96,128,160,192,224,256,288,320,352,384,416,448,480,0},{48,80,112..., dimensions={0} | all-to-all | bytes 1048576 | tf_op jit(solution)/shard_map/all_to_all | solution.py:326
  33.5 0.0 collective-permute-done.1.got
  33.5 0.0 copy-done
  33.5 0.0 copy-done.1
  33.5 0.0 copy-done.2
  33.5 3.3 %attend.1 = bf16[16,144,128]{2,1,0:T(8,128)(2,1)S(1)} custom-call(s32[4]{0:T(128)S(1)} %copy-done, s32[4]{0:T(128)S(1)} %copy-done.1, s32[16]{0:T(128)S(1)} %copy-done.2, bf16[16,128,128]{2,1,0:T(8,128)(2,1)S(1)} %all_to_all.15.queries, bf16[4,336,1024]{2,1,0:T(8,128)(2,1)S(1)} %stage.1.held, bf16[4,336,1024]{2,1,0:T(8,128)(2,1)S(1)} %collective-permute-done.1.got), custom_call_target="tpu_custom_call" | custom-call | tf_op jit(solution)/shard_map/attend/pallas_call | solution.py:330
  36.8 13.7 %all_to_all.16.got = bf16[16,144,128]{2,1,0:T(8,128)(2,1)S(1)} all-to-all(bf16[16,144,128]{2,1,0:T(8,128)(2,1)S(1)} %attend.1), channel_id=1, replica_groups={{320,352,384,416,448,480,0,32,64,96,128,160,192,224,256,288},{336,368,4..., dimensions={0} | all-to-all | bytes 1179648 | tf_op jit(solution)/shard_map/all_to_all | solution.py:342
  50.5 0.4 plane.1
  51.0 16.0 %all_to_all.17.got = bf16[16,16,128]{2,1,0:T(8,128)(2,1)S(1)} all-to-all(bf16[16,16,128]{2,1,0:T(8,128)(2,1)S(1)} %plane.1), channel_id=1, replica_groups={{8,9,10,11,12,13,14,15,0,1,2,3,4,5,6,7},{24,25,26,27,28,29,30,31,16,17,..., dimensions={0} | all-to-all | bytes 131072 | tf_op jit(solution)/shard_map/all_to_all | solution.py:351
  67.0 0.8 %final.1 = bf16[4,256]{1,0:T(4,128)(2,1)} custom-call(bf16[16,16,128]{2,1,0:T(8,128)(2,1)S(1)} %all_to_all.17.got), custom_call_target="tpu_custom_call" | custom-call | tf_op jit(solution)/shard_map/final/pallas_call | solution.py:352
Async XLA Ops:
  2.6 15.6 %collective-permute-start = (bf16[128,128]{1,0:T(8,128)(2,1)S(1)}, bf16[128,128]{1,0:T(8,128)(2,1)S(1)}, u32[]{:S(2)}, u32[]{:S(2)}) collective-permute-start(bf16[128,128]{1,0:T(8,128)(2,1)S(1)} %get-tuple-element.7), channel_id=1, source_target_pairs={{0,8},{1,9},{2,10},{3,11},{4,12},{5,13},{6,14},{7,15},{8,0},{9,1},... | collective-permute-start | bytes 98312 | tf_op jit(solution)/shard_map/ppermute | solution.py:311
  14.2 19.3 %copy-start = (s32[4]{0:T(128)S(1)}, s32[4]{0:T(128)}, u32[]{:S(2)}) copy-start(s32[4]{0:T(128)} %page_prompt.5) | copy-start | bytes 52
  14.2 19.3 %copy-start.1 = (s32[4]{0:T(128)S(1)}, s32[4]{0:T(128)}, u32[]{:S(2)}) copy-start(s32[4]{0:T(128)} %suffix_len.1) | copy-start | bytes 52
  14.2 19.3 %copy-start.2 = (s32[16]{0:T(128)S(1)}, s32[16]{0:T(128)}, u32[]{:S(2)}) copy-start(s32[16]{0:T(128)} %constant.2.clone.chip_of) | copy-start | bytes 196
  14.2 19.3 %collective-permute-start.1 = (bf16[4,336,1024]{2,1,0:T(8,128)(2,1)S(1)}, bf16[4,336,1024]{2,1,0:T(8,128)(2,1)S(1)}, u32[]{:S(2)}, u32[]{:S(2)}) collective-permute-start(bf16[4,336,1024]{2,1,0:T(8,128)(2,1)S(1)} %stage.1.held), channel_id=1, source_target_pairs={{0,16},{16,0},{32,48},{48,32},{64,80},{80,64},{96,112},{112,96},{1... | collective-permute-start | bytes 8257544 | tf_op jit(solution)/shard_map/ppermute | solution.py:315

commit v7 on v6

--- a/solution.py
+++ b/solution.py
@@ -35,10 +35,10 @@
 CHIP_ORDER = (0, 4, 1, 2, 8, 3, 12, 5, 6, 9, 13, 7, 14, 11, 10, 15)
 DISTANCES = (8, 7, 9, 6, 10, 5, 11, 4, 12, 3, 13, 2, 14, 1, 15, 0)
 DISTANCE_OF = dict(zip(CHIP_ORDER, DISTANCES))
-CHIP_GROUP = tuple(range(10, PLANE)) + tuple(range(10))
+SUM_FIRST = (10, 0)
+QUERY_FIRST = (1, 11)
 PLANE_GROUP = tuple(range(8, DEPTH)) + tuple(range(8))
-QUERY_GROUP = tuple(range(1, PLANE)) + tuple(range(1))
-CHIP_OF = {distance: QUERY_GROUP.index(chip) for distance, chip in zip(DISTANCES, CHIP_ORDER)}
+CHIP_OF = dict(zip(DISTANCES, CHIP_ORDER))
 EARLY_PLANES = 7
 F32 = jnp.float32
 BF16 = jnp.bfloat16
@@ -108,7 +108,10 @@
     top, peak, total, acc = (buffers[i * KVH:(i + 1) * KVH] for i in range(4))
     prefix = lax.axis_index("prefix")
     plane = lax.axis_index("sample")
-    sign = 1 - 2 * lax.rem(prefix, CORES)
+    core = lax.rem(prefix, CORES)
+    sign = 1 - 2 * core
+    query_first = jnp.where(core == 0, QUERY_FIRST[0], QUERY_FIRST[1])
+    sum_first = jnp.where(core == 0, SUM_FIRST[0], SUM_FIRST[1])
     for a in range(KVH):
         top[a][:PROMPTS] = jnp.full((PROMPTS, HEAD_ROWS, HD), NEG, F32)
         total[a][:PROMPTS] = jnp.zeros((PROMPTS, HEAD_ROWS, HD), F32)
@@ -138,7 +141,7 @@
 
     def chip_rows(sample_plane, a):
         chip = chip_of[(sign * (plane - sample_plane)) & (DEPTH - 1)]
-        return queries[chip, pl.ds(a * 16, 16), :]
+        return queries[(chip - query_first) & (PLANE - 1), pl.ds(a * 16, 16), :]
 
     def query_rows(prompt, a):
         return jnp.concatenate([chip_rows(prompt * 4 + q, a) for q in range(4)], axis=0)
@@ -203,7 +206,7 @@
         for half in range(2):
             def quarter_rows(tile, q):
                 return tile[q * 16 + half * 8:q * 16 + half * 8 + 8]
-            owner = CHIP_GROUP.index(a * 2 + half)
+            owner = (a * 2 + half - sum_first) & (PLANE - 1)
             for prompt in range(PROMPTS):
                 sums = acc[a][prompt]
                 rows = jnp.concatenate([quarter_rows(sums, q) for q in range(4)], axis=0)
@@ -276,6 +279,11 @@
     return pltpu.CompilerParams(vmem_limit_bytes=int(mib * MIB))
 
 
+def chip_groups(first):
+    return [[(first[core] + i) % PLANE * CORES + core for i in range(PLANE)]
+            for core in range(CORES)]
+
+
 def body(queries, pool_keys, pool_values, page_prompt, suffix_keys, suffix_values, suffix_len):
     def pages():
         return tuple(
@@ -313,7 +321,6 @@
         [((chip * CORES + core) * DEPTH + z, (chip * CORES + core) * DEPTH + (z + (1 - 2 * core) * DISTANCE_OF[chip]) % DEPTH)
          for chip in range(PLANE) for core in range(CORES) for z in range(DEPTH)])
     got = lax.ppermute(held, "prefix", [(i, i ^ 1) for i in range(CORES * PLANE)])
-    same_core = [[chip * CORES + core for chip in CHIP_GROUP] for core in range(CORES)]
     copies = pl.pallas_call(
         copy_kernel,
         out_shape=jax.ShapeDtypeStruct((PLANE, ROWS, HD), BF16),
@@ -324,8 +331,7 @@
         name="copies",
     )(shifted)
     every_query = lax.all_to_all(
-        copies, "prefix", 0, 0,
-        axis_index_groups=[[chip * CORES + core for chip in QUERY_GROUP] for core in range(CORES)])
+        copies, "prefix", 0, 0, axis_index_groups=chip_groups(QUERY_FIRST))
     chip_of = jnp.array([CHIP_OF[distance] for distance in range(DEPTH)], jnp.int32)
     partial = pl.pallas_call(
         attend_kernel,
@@ -339,7 +345,7 @@
         compiler_params=budget(18),
         name="attend",
     )(page_prompt, suffix_len, chip_of, every_query, held, got)
-    partial = lax.all_to_all(partial, "prefix", 0, 0, axis_index_groups=same_core)
+    partial = lax.all_to_all(partial, "prefix", 0, 0, axis_index_groups=chip_groups(SUM_FIRST))
     summed = pl.pallas_call(
         plane_kernel,
         out_shape=jax.ShapeDtypeStruct((DEPTH, 16, HD), BF16),

time: 68.1 us -> 72.8 us (1.069)
  the two profiles are of different devices: /device:TPU:2 before, /device:TPU:1 now
where the time goes in v7:
time: 72.8 us; the launch traced here: 72.5 us
  blocking collectives  47.4 us (65%)
  starting transfers between devices  17.6 us (24%)
  Pallas kernels  7.38 us (10%)
    all_to_all x1, blocking collectives, body(): lax.all_to_all(partial, 'prefix', 0, 0, axis_index_groups=chip_groups(SUM...  18 us
    all_to_all x1, blocking collectives, body(): lax.all_to_all(summed, 'sample', 0, 0, axis_index_groups=[list(PLANE_GROU...  16.5 us
    ppermute x1, starting transfers between devices, body(): lax.ppermute(own_queries, ('prefix', 'sample'), [((chip * CORES + core) *...  14.6 us
    all_to_all x1, blocking collectives, body(): lax.all_to_all(copies, 'prefix', 0, 0, axis_index_groups=chip_groups(QUER...  12.8 us
    pallas_call x1, Pallas kernels, body(): pl.pallas_call(attend_kernel, out_shape=jax.ShapeDtypeStruct((PLANE, BLOC...  3.37 us
    ppermute x1, starting transfers between devices, body(): lax.ppermute(held, 'prefix', [(i, i ^ 1) for i in range(CORES * PLANE)])  3 us
    pallas_call x1, Pallas kernels, body(): pl.pallas_call(query_kernel, out_shape=(jax.ShapeDtypeStruct((ROWS, HD),...  2.6 us
  transfers between devices with their start and end apart: 2, of which 0 were waited for; matrix products, arithmetic and copies ran while one was open for 0% of the time, Pallas kernels for 0%

profile of v7, /device:TPU:1, one launch (start us, length us, event | category | flops | bytes accessed | tf_op | source)
XLA Modules:
  0.0 72.5 jit_solution(6035434010686304869)
XLA Ops:
  0.0 2.6 %query.1 = (bf16[128,128]{1,0:T(8,128)(2,1)S(1)}, bf16[4,336,1024]{2,1,0:T(8,128)(2,1)S(1)}) custom-call(bf16[4,8192]{1,0:T(4,128)(2,1)} %queries_hbm.1, s32[4]{0:T(128)} %page_prompt.5, bf16[4,128,1024]{2,1,0:T(8,128)(2,1)} %pool_keys.3, bf16[4,128,1024]{2,1,0:T(8,128)(2,1)} %pool_values.3, bf16[4,32,1024]{2,1,0:T(8,128)(2,1)} %suffix_keys.3, ...), custom_call_target="tpu_custom_call" | custom-call | tf_op jit(solution)/shard_map/query/pallas_call | solution.py:300
  2.6 14.6 %collective-permute-start = (bf16[128,128]{1,0:T(8,128)(2,1)S(1)}, bf16[128,128]{1,0:T(8,128)(2,1)S(1)}, u32[]{:S(2)}, u32[]{:S(2)}) collective-permute-start(bf16[128,128]{1,0:T(8,128)(2,1)S(1)} %get-tuple-element.7), channel_id=1, source_target_pairs={{0,8},{1,9},{2,10},{3,11},{4,12},{5,13},{6,14},{7,15},{8,0},{9,1},... | collective-permute-start | bytes 98312 | tf_op jit(solution)/shard_map/ppermute | solution.py:319
  17.2 0.1 stage.1.held
  17.3 0.0 copy-start
  17.3 0.0 copy-start.1
  17.3 0.0 copy-start.2
  17.3 3.0 %collective-permute-start.1 = (bf16[4,336,1024]{2,1,0:T(8,128)(2,1)S(1)}, bf16[4,336,1024]{2,1,0:T(8,128)(2,1)S(1)}, u32[]{:S(2)}, u32[]{:S(2)}) collective-permute-start(bf16[4,336,1024]{2,1,0:T(8,128)(2,1)S(1)} %stage.1.held), channel_id=1, source_target_pairs={{0,16},{16,0},{32,48},{48,32},{64,80},{80,64},{96,112},{112,96},{1... | collective-permute-start | bytes 8257544 | tf_op jit(solution)/shard_map/ppermute | solution.py:323
  20.3 0.0 collective-permute-done.shifted
  20.3 0.1 copies.1
  20.4 12.8 %all_to_all.15.queries = bf16[16,128,128]{2,1,0:T(8,128)(2,1)S(1)} all-to-all(bf16[16,128,128]{2,1,0:T(8,128)(2,1)S(1)} %copies.1), channel_id=1, replica_groups={{32,64,96,128,160,192,224,256,288,320,352,384,416,448,480,0},{368,400,4..., dimensions={0} | all-to-all | bytes 1048576 | tf_op jit(solution)/shard_map/all_to_all | solution.py:333
  33.3 0.0 collective-permute-done.1.got
  33.3 0.0 copy-done
  33.3 0.0 copy-done.1
  33.3 0.0 copy-done.2
  33.3 3.4 %attend.1 = bf16[16,144,128]{2,1,0:T(8,128)(2,1)S(1)} custom-call(s32[4]{0:T(128)S(1)} %copy-done, s32[4]{0:T(128)S(1)} %copy-done.1, s32[16]{0:T(128)S(1)} %copy-done.2, bf16[16,128,128]{2,1,0:T(8,128)(2,1)S(1)} %all_to_all.15.queries, bf16[4,336,1024]{2,1,0:T(8,128)(2,1)S(1)} %stage.1.held, bf16[4,336,1024]{2,1,0:T(8,128)(2,1)S(1)} %collective-permute-done.1.got), custom_call_target="tpu_custom_call" | custom-call | tf_op jit(solution)/shard_map/attend/pallas_call | solution.py:336
  36.7 18.0 %all_to_all.16.got = bf16[16,144,128]{2,1,0:T(8,128)(2,1)S(1)} all-to-all(bf16[16,144,128]{2,1,0:T(8,128)(2,1)S(1)} %attend.1), channel_id=1, replica_groups={{320,352,384,416,448,480,0,32,64,96,128,160,192,224,256,288},{16,48,80,..., dimensions={0} | all-to-all | bytes 1179648 | tf_op jit(solution)/shard_map/all_to_all | solution.py:348
  54.7 0.4 plane.1
  55.1 16.5 %all_to_all.17.got = bf16[16,16,128]{2,1,0:T(8,128)(2,1)S(1)} all-to-all(bf16[16,16,128]{2,1,0:T(8,128)(2,1)S(1)} %plane.1), channel_id=1, replica_groups={{8,9,10,11,12,13,14,15,0,1,2,3,4,5,6,7},{24,25,26,27,28,29,30,31,16,17,..., dimensions={0} | all-to-all | bytes 131072 | tf_op jit(solution)/shard_map/all_to_all | solution.py:357
  71.7 0.8 %final.1 = bf16[4,256]{1,0:T(4,128)(2,1)} custom-call(bf16[16,16,128]{2,1,0:T(8,128)(2,1)S(1)} %all_to_all.17.got), custom_call_target="tpu_custom_call" | custom-call | tf_op jit(solution)/shard_map/final/pallas_call | solution.py:358
Async XLA Ops:
  2.6 17.7 %collective-permute-start = (bf16[128,128]{1,0:T(8,128)(2,1)S(1)}, bf16[128,128]{1,0:T(8,128)(2,1)S(1)}, u32[]{:S(2)}, u32[]{:S(2)}) collective-permute-start(bf16[128,128]{1,0:T(8,128)(2,1)S(1)} %get-tuple-element.7), channel_id=1, source_target_pairs={{0,8},{1,9},{2,10},{3,11},{4,12},{5,13},{6,14},{7,15},{8,0},{9,1},... | collective-permute-start | bytes 98312 | tf_op jit(solution)/shard_map/ppermute | solution.py:319
  17.3 16.0 %copy-start = (s32[4]{0:T(128)S(1)}, s32[4]{0:T(128)}, u32[]{:S(2)}) copy-start(s32[4]{0:T(128)} %page_prompt.5) | copy-start | bytes 52
  17.3 16.0 %copy-start.1 = (s32[4]{0:T(128)S(1)}, s32[4]{0:T(128)}, u32[]{:S(2)}) copy-start(s32[4]{0:T(128)} %suffix_len.1) | copy-start | bytes 52
  17.3 16.0 %copy-start.2 = (s32[16]{0:T(128)S(1)}, s32[16]{0:T(128)}, u32[]{:S(2)}) copy-start(s32[16]{0:T(128)} %constant.2.clone.chip_of) | copy-start | bytes 196
  17.3 15.9 %collective-permute-start.1 = (bf16[4,336,1024]{2,1,0:T(8,128)(2,1)S(1)}, bf16[4,336,1024]{2,1,0:T(8,128)(2,1)S(1)}, u32[]{:S(2)}, u32[]{:S(2)}) collective-permute-start(bf16[4,336,1024]{2,1,0:T(8,128)(2,1)S(1)} %stage.1.held), channel_id=1, source_target_pairs={{0,16},{16,0},{32,48},{48,32},{64,80},{80,64},{96,112},{112,96},{1... | collective-permute-start | bytes 8257544 | tf_op jit(solution)/shard_map/ppermute | solution.py:323
